TPU v7x, 128 devices: a whole 4x4x4 slice. The times are simulated.
128 devices in a mesh: lon: 16 (over x_lo, y, core), lat: 8 (over z, x_hi).
Axes of the slice: x: 4 (x_hi: 2, x_lo: 2; x = x_hi * 2 + x_lo), y: 4, z: 4, core: 2. Of those that a mesh axis runs over, the one named last changes fastest.
Arguments:
- field: bfloat16 [192, 48, 8, 192], P('lon', 'lat'), may hold values from -6 to 6
- w_qkv: bfloat16 [192, 576], replicated, may hold values from -0.4375 to 0.4375
- w_proj: bfloat16 [192, 192], replicated, may hold values from -0.4375 to 0.4375
- w_fc1: bfloat16 [192, 768], replicated, may hold values from -0.4375 to 0.4375
- w_fc2: bfloat16 [768, 192], replicated, may hold values from -0.21875 to 0.21875
- bias_table: float32 [8, 4, 6, 3312], P('lat'), may hold values from -4 to 342
- cotangent: bfloat16 [192, 48, 8, 192], P('lon', 'lat'), may hold values from -6 to 6
Outputs:
- out_field: bfloat16 [192, 48, 8, 192], P('lon', 'lat')
- grad_field: bfloat16 [192, 48, 8, 192], P('lon', 'lat')
- grad_qkv: float32 [192, 576], replicated
- grad_proj: float32 [192, 192], replicated
- grad_fc1: float32 [192, 768], replicated
- grad_fc2: float32 [768, 192], replicated
- grad_bias: float32 [8, 4, 6, 3312], P('lat')
All inputs are finite; a program needn't handle non-finite values.
Results may differ from a plain program's by a relative error of at most 0.029.
Values may be sent and summed in bfloat16 or wider, within the bound.
A program may use at most 192 MiB of HBM per device.

v0:
```python
import jax
import jax.numpy as jnp
from jax import lax
from jax.sharding import PartitionSpec as P

WLON = 12
WLAT = 6
WLEV = 2


EPSILON = 1e-05
MASKED = -1000000000.0


def as_sent(value):
    return jax.tree.map(lambda a: a.astype(jnp.bfloat16) if a.dtype == jnp.float32 else a, value)


def passed_along(block, axis, distance):
    devices = range(lax.axis_size(axis))
    route = [((i - distance) % len(devices), i) for i in devices]
    return lax.ppermute(block, axis, route)


def layer_norm(tiles):
    widened = tiles.astype(jnp.float32)
    centered = widened - jnp.mean(widened, axis=-1, keepdims=True)
    spread = jnp.mean(centered * centered, axis=-1, keepdims=True)
    return (centered * lax.rsqrt(spread + EPSILON)).astype(jnp.bfloat16)


def to_windows(tiles):
    lon_len, lat_len, levels, features = tiles.shape
    shaped = tiles.reshape(
        lon_len // WLON, WLON, lat_len // WLAT, WLAT, levels // WLEV, WLEV, features
    )
    shaped = shaped.transpose(2, 4, 0, 5, 3, 1, 6)
    return shaped.reshape(
        lat_len // WLAT, levels // WLEV, lon_len // WLON, WLEV * WLAT * WLON, features
    )


def from_windows(blocks, lon_len, lat_len):
    lat_win, lev_win, lon_win, window_len, features = blocks.shape
    shaped = blocks.reshape(lat_win, lev_win, lon_win, WLEV, WLAT, WLON, features)
    shaped = shaped.transpose(2, 5, 0, 4, 1, 3, 6)
    return shaped.reshape(lon_len, lat_len, lev_win * WLEV, features)


def expand_bias(table):
    lat_win, lev_win, head_count, positions = table.shape
    shaped = table.reshape(lat_win, lev_win, head_count, WLEV, WLEV, WLAT, WLAT, 2 * WLON - 1)
    stacked = jnp.stack(
        [shaped[..., offset : offset + WLON][..., ::-1] for offset in range(WLON)], axis=-2
    )
    stacked = stacked.transpose(0, 1, 2, 3, 5, 7, 4, 6, 8)
    window_len = WLEV * WLAT * WLON
    return stacked.reshape(lat_win, lev_win, head_count, window_len, window_len)


def window_groups(last_lat, lev_win):
    token_ids = jnp.arange(WLEV * WLAT * WLON)
    level_place = token_ids // (WLAT * WLON)
    lat_place = token_ids // WLON % WLAT
    lat_group = jnp.where(last_lat[:, None] & (lat_place[None, :] >= WLAT // 2), 2, 0)
    lev_last = jnp.arange(lev_win) == lev_win - 1
    lev_group = jnp.where(lev_last[:, None] & (level_place[None, :] >= WLEV // 2), 1, 0)
    group = lat_group[:, None, :] + lev_group[None, :, :]
    return group[:, :, :, None] == group[:, :, None, :]


def forward_block(tokens, probes, weights, bias, allowed):
    w_qkv, w_proj, w_fc1, w_fc2 = weights
    probe_qkv, probe_scores, probe_proj, probe_fc1, probe_fc2 = probes
    lon_len, lat_len, levels, features = tokens.shape
    head_count = bias.shape[2]
    head_dim = features // head_count
    row_count = lon_len * lat_len * levels
    normed = layer_norm(tokens).reshape(row_count, features)
    qkv = (jnp.dot(normed, w_qkv, preferred_element_type=jnp.float32) + probe_qkv).astype(
        jnp.bfloat16
    )
    windows = to_windows(qkv.reshape(lon_len, lat_len, levels, 3 * features))
    lead_shape = windows.shape[:4]
    queries = windows[..., :features].reshape(lead_shape + (head_count, head_dim))
    key_part = windows[..., features : 2 * features].reshape(lead_shape + (head_count, head_dim))
    value_part = windows[..., 2 * features :].reshape(lead_shape + (head_count, head_dim))
    scores = jnp.einsum(
        "avonhd,avomhd->avohnm", queries, key_part, preferred_element_type=jnp.float32
    )
    scores = scores * (1.0 / jnp.sqrt(jnp.float32(head_dim)))
    scores = scores + bias[:, :, None] + probe_scores
    scores = jnp.where(allowed[:, :, None, None], scores, MASKED)
    highest = jnp.max(scores, axis=-1, keepdims=True)
    exponent = jnp.exp(scores - highest)
    soft_weights = (exponent / jnp.sum(exponent, axis=-1, keepdims=True)).astype(jnp.bfloat16)
    blended = jnp.einsum(
        "avohnm,avomhd->avonhd", soft_weights, value_part, preferred_element_type=jnp.float32
    ).astype(jnp.bfloat16)
    blended = from_windows(blended.reshape(lead_shape + (features,)), lon_len, lat_len).reshape(
        row_count, features
    )
    projected = jnp.dot(blended, w_proj, preferred_element_type=jnp.float32) + probe_proj
    middle = (tokens.reshape(row_count, features).astype(jnp.float32) + projected).astype(
        jnp.bfloat16
    )
    normed_two = layer_norm(middle)
    first_product = jnp.dot(normed_two, w_fc1, preferred_element_type=jnp.float32) + probe_fc1
    hidden = jax.nn.gelu(first_product, approximate=False).astype(jnp.bfloat16)
    second_product = jnp.dot(hidden, w_fc2, preferred_element_type=jnp.float32) + probe_fc2
    result = (middle.astype(jnp.float32) + second_product).astype(jnp.bfloat16)
    return (result.reshape(tokens.shape), (normed, blended, normed_two, hidden))


def contract(left_rows, right_rows):
    return jnp.einsum(
        "tc,tk->ck", left_rows, right_rows.astype(jnp.bfloat16), preferred_element_type=jnp.float32
    )


def local_pass(tokens, upstream, weights, bias_table, last_lat, first_col):
    lon_len, lat_len, levels, features = tokens.shape
    row_count = lon_len * lat_len * levels
    bias, expand_back = jax.vjp(expand_bias, bias_table)
    lat_win, lev_win, head_count, window_len = bias.shape[:4]
    allowed = window_groups(last_lat, lev_win)
    hidden_units = weights[2].shape[1]
    probes = (
        jnp.zeros((row_count, 3 * features), jnp.float32),
        jnp.zeros(
            (lat_win, lev_win, lon_len // WLON, head_count, window_len, window_len), jnp.float32
        ),
        jnp.zeros((row_count, features), jnp.float32),
        jnp.zeros((row_count, hidden_units), jnp.float32),
        jnp.zeros((row_count, features), jnp.float32),
    )

    def apply(lattice, extra):
        return forward_block(lattice, extra, weights, bias, allowed)

    result, pullback, saved = jax.vjp(apply, tokens, probes, has_aux=True)
    grad_tokens, grad_probes = pullback(upstream)
    normed, blended, normed_two, hidden = saved
    start = first_col * lat_len * levels
    grads = (
        contract(normed[start:], grad_probes[0][start:]),
        contract(blended[start:], grad_probes[2][start:]),
        contract(normed_two[start:], grad_probes[3][start:]),
        contract(hidden[start:], grad_probes[4][start:]),
    )
    score_grad = jnp.sum(grad_probes[1][:, :, first_col // WLON :], axis=2)
    (grad_bias,) = expand_back(score_grad)
    return (result, grad_tokens, grads, grad_bias)


def lon_move(portion, offset):
    return passed_along(as_sent(portion), "lon", offset).astype(portion.dtype)


def lat_move(portion, offset):
    return passed_along(as_sent(portion), "lat", offset).astype(portion.dtype)


def roll_inward(tiles):
    half_rows = WLAT // 2
    moved = jnp.concatenate([tiles[:, half_rows:], lat_move(tiles[:, :half_rows], -1)], axis=1)
    return jnp.roll(moved, -(WLEV // 2), axis=2)


def roll_outward(tiles):
    half_rows = WLAT // 2
    moved = jnp.roll(tiles, WLEV // 2, axis=2)
    return jnp.concatenate([lat_move(moved[:, -half_rows:], 1), moved[:, :-half_rows]], axis=1)


def per_device(field, w_qkv, w_proj, w_fc1, w_fc2, bias_table, cotangent):
    weights = (w_qkv, w_proj, w_fc1, w_fc2)
    half_cols = WLON // 2
    last_band = lax.axis_index("lat") == lax.axis_size("lat") - 1
    lat_win = bias_table.shape[0]
    last_lat = (jnp.arange(lat_win) == lat_win - 1) & last_band
    tokens = jnp.concatenate([field[half_cols:], lon_move(field[:half_cols], -1)], axis=0)
    upstream = jnp.concatenate([cotangent[half_cols:], lon_move(cotangent[:half_cols], -1)], axis=0)
    first_col = 0
    result, grad_tokens, grads, grad_bias = local_pass(
        roll_inward(tokens), roll_inward(upstream), weights, bias_table, last_lat, first_col
    )
    result = roll_outward(result)
    grad_tokens = roll_outward(grad_tokens)
    out_field = jnp.concatenate([lon_move(result[-half_cols:], 1), result[:-half_cols]], axis=0)
    grad_field = jnp.concatenate(
        [lon_move(grad_tokens[-half_cols:], 1), grad_tokens[:-half_cols]], axis=0
    )
    summed = lax.psum((grads[0], grads[1], grads[2], grads[3]), ("lon", "lat"))
    bias_total = lax.psum(grad_bias.astype(jnp.bfloat16), "lon").astype(jnp.float32)
    return (out_field, grad_field, summed[0], summed[1], summed[2], summed[3], bias_total)


def solution(mesh):
    in_specs = (
        P("lon", "lat", None, None),
        P(),
        P(),
        P(),
        P(),
        P("lat", None, None, None),
        P("lon", "lat", None, None),
    )
    out_specs = (
        P("lon", "lat", None, None),
        P("lon", "lat", None, None),
        P(),
        P(),
        P(),
        P(),
        P("lat", None, None, None),
    )
    return jax.shard_map(
        per_device, mesh=mesh, in_specs=in_specs, out_specs=out_specs, check_vma=False
    )
```

profile of v0, /device:TPU:1, one launch (start us, length us, event | category | flops | bytes accessed | tf_op | source)
XLA Modules:
  0.0 647.7 jit_solution(14741396211459085511)
XLA Ops:
  11.4 3.5 collective-permute-start.4
  17.6 12.8 %fusion.64 = (f32[1,4,6,2,2,6,6,12]{7,6,5,4,3,1,2,0:T(8,128)}, f32[1,4,6,2,2,6,6,12]{7,6,5,4,3,1,2,0:T(8,128)}, f32[1,4,6,2,2,6,6,12]{7,6,5,4,3,1,2,0:T(8,128)},...) fusion(f32[1,4,6,2,2,6,6,23]{7,6,5,4,3,1,2,0:T(8,128)S(1)} %res, ...), kind=kLoop, calls=%fused_computation.167 | loop fusion | bytes 3981312 | tf_op jit(solution)/shard_map/jvp()/slice | solution.py:54
  30.3 5.4 rev.72
  35.7 4.0 bitcast_dynamic-update-slice_fusion.11
  42.9 5.5 rev.74
  51.7 5.6 rev.76
  60.5 5.5 rev.78
  69.2 5.5 rev.80
  78.0 5.5 rev.82
  86.9 3.9 bitcast_dynamic-update-slice_fusion.10
  112.5 43.5 %copy.105 = f32[1,4,6,2,6,12,2,6,12]{5,4,3,8,7,6,2,1,0:T(8,128)} copy(f32[1,4,6,2,6,12,2,6,12]{8,6,7,4,3,2,1,5,0:T(2,128)} %bitcast.160) | data formatting | bytes 3981312 | tf_op jit(solution)/shard_map/jvp()/broadcast_in_dim;jvp()/reshape | solution.py:92
  156.1 19.7 %reshape.502 = f32[4,6,144,144]{2,3,1,0:T(8,128)} reshape(f32[1,4,6,2,6,12,2,6,12]{5,4,3,8,7,6,2,1,0:T(8,128)} %copy.105) | data formatting | bytes 3981312 | tf_op jit(solution)/shard_map/jvp()/broadcast_in_dim;jvp()/reshape | solution.py:92
  176.8 6.0 collective-permute-start.1
  203.0 5.4 multiply_convert_fusion
  229.0 5.9 copy.87
  251.4 18.4 %reshape.499 = f32[1,4,6,2,6,12,2,6,12]{8,7,6,5,4,3,2,1,0:T(8,128)} reshape(f32[4,6,144,144]{3,2,1,0:T(8,128)} %copy.87) | data formatting | bytes 3981312 | tf_op jit(solution)/shard_map/transpose(jvp())/reshape | solution.py:58
  269.9 18.7 %slice_bitcast_fusion.11 = (f32[1,4,6,2,2,6,6,12]{7,6,4,5,3,2,1,0:T(8,128)}, f32[1,4,6,2,2,6,6,12]{7,6,4,5,3,2,1,0:T(8,128)}, f32[1,4,6,2,2,6,6,12]{7,6,4,5,3,2,...) fusion(f32[1,4,6,2,2,6,6,12,12]{8,6,4,7,5,3,2,1,0:T(8,128)} %bi, ...), kind=kLoop, calls=%fused_computation.27 | loop fusion | bytes 3981312 | tf_op jit(solution)/shard_map/transpose(jvp())/unstack | solution.py:53
  288.6 5.4 rev.84
  294.0 5.4 rev.85
  299.4 5.4 rev.86
  304.8 5.4 rev.87
  310.3 5.4 rev.88
  315.7 5.4 rev.89
  321.1 5.4 rev.90
  326.5 5.4 rev.91
  331.9 5.4 rev.92
  337.4 5.4 rev.93
  342.8 5.4 rev.94
  351.4 12.7 %add_convert_fusion = bf16[1,4,6,2,2,6,6,23]{7,6,4,5,3,2,1,0:T(8,128)(2,1)S(1)} fusion(f32[1,4,6,2,2,6,6,12]{7,6,4,5,3,2,1,0:T(8,128)} %rev.95, f32[1,4,6,2,2,6,6,12]{7,6,4,5,3,2,1,0:T(8,128)} %rev.94, f32[1,4,6,2,2,6,6,12]{7,6,4,5,3,2,1,0:T(8,128)} %rev.93, f32[1,4,6,2,2,6,6,12]{7,6,4,5,3,2,1,0:T(8,128)} %rev.92, f32[1,4,6,2,2,6,6,12]{7,6,4,5,3,2,1,0:T(8,128)} %rev.91, ...), kind=kLoop, calls=%fused_computation.28 | loop fusion | flops 953856 | bytes 2149632 | tf_op jit(solution)/shard_map/convert_element_type | solution.py:195
  371.9 5.1 collective-permute-done.6
  381.4 92.8 %all-reduce.19.cloned.1.call-done = bf16[1,4,6,3312]{3,1,2,0:T(4,128)(2,1)} async-done(((bf16[1,4,6,3312]{3,1,2,0:T(4,128)(2,1)}), bf16[1,4,6,3312]{3,1,2,0:T(4,128)(2,1)}) %all-reduce.19.cloned.1.call-update) | async-done | bytes 158992 | tf_op jit(solution)/shard_map/psum | solution.py:195
  477.3 157.1 %all-reduce.21.cloned.1.call-done = (f32[192,576]{1,0:T(8,128)}, f32[192,192]{1,0:T(8,128)}, f32[192,768]{1,0:T(8,128)}, f32[768,192]{0,1:T(8,128)}) async-done(((f32[192,576]{1,0:T(8,128)}, f32[192,192]{1,0:T(8,128)}, f32[192,768]{1,0:T(8,128)}, f32[768,192]{0,1:T(8,128)}), (f32[192,576]{1,0:T(8,128)}, f32[192,192]{1,0:T(8,128)}, f32[192,768]{1,0:T(8,128)}, ...) | async-done | bytes 1769488 | tf_op jit(solution)/shard_map/psum | solution.py:194
  (258 shorter events, 130.3 us)
Async XLA Ops:
  7.2 195.8 %copy-start = (bf16[192,768]{1,0:T(8,128)(2,1)S(1)}, bf16[192,768]{1,0:T(8,128)(2,1)}, u32[]{:S(2)}) copy-start(bf16[192,768]{1,0:T(8,128)(2,1)} %param.10) | copy-start | bytes 884740
  7.2 467.0 %all-reduce.19.cloned.1.call-start = ((), (), s32[]{:S(2)}) async-start(), calls=%async_computation | async-start | bytes 319488 | tf_op jit(solution)/shard_map/psum | solution.py:195
  8.9 166.8 %collective-permute-start = (bf16[6,6,8,192]{3,2,1,0:T(8,128)(2,1)}, bf16[6,6,8,192]{3,2,1,0:T(8,128)(2,1)}, u32[]{:S(2)}, u32[]{:S(2)}) collective-permute-start(bf16[6,6,8,192]{3,2,1,0:T(8,128)(2,1)} %get-tuple-element.56), channel_id=1, source_target_pairs={{8,0},{16,8},{24,16},{32,24},{40,32},{48,40},{56,48},{64,56},{72,6... | collective-permute-start | bytes 331784 | tf_op jit(solution)/shard_map/ppermute | solution.py:22
  11.4 171.4 %collective-permute-start.4 = (bf16[6,6,8,192]{3,2,1,0:T(8,128)(2,1)S(1)}, bf16[6,6,8,192]{3,2,1,0:T(8,128)(2,1)S(1)}, u32[]{:S(2)}, u32[]{:S(2)}) collective-permute-start(bf16[6,6,8,192]{3,2,1,0:T(8,128)(2,1)S(1)} %get-tuple-element.50), channel_id=1, source_target_pairs={{8,0},{16,8},{24,16},{32,24},{40,32},{48,40},{56,48},{64,56},{72,6... | collective-permute-start | bytes 331784 | tf_op jit(solution)/shard_map/ppermute | solution.py:22
  42.9 5.5 copy-start.14
  51.7 5.6 copy-start.13
  60.5 5.5 copy-start.12
  69.2 5.5 copy-start.11
  78.0 5.5 copy-start.10
  112.5 76.2 %copy-start.41 = (pred[4,144,144]{1,2,0:T(8,128)(4,1)}, pred[4,144,144]{1,2,0:T(8,128)(4,1)S(1)}, u32[]{:S(2)}) copy-start(pred[4,144,144]{1,2,0:T(8,128)(4,1)S(1)} %broadcast_compare_fusion.1) | copy-start | bytes 248836
  175.8 10.9 %copy-start.48 = (bf16[192,576]{1,0:T(8,128)(2,1)S(1)}, bf16[192,576]{1,0:T(8,128)(2,1)}, u32[]{:S(2)}) copy-start(bf16[192,576]{1,0:T(8,128)(2,1)} %param.8) | copy-start | bytes 663556
  176.8 8.8 %collective-permute-start.1 = (bf16[12,3,8,192]{3,2,1,0:T(8,128)(2,1)S(1)}, bf16[12,3,8,192]{3,2,1,0:T(8,128)(2,1)S(1)}, u32[]{:S(2)}, u32[]{:S(2)}) collective-permute-start(bf16[12,3,8,192]{3,2,1,0:T(8,128)(2,1)S(1)} %get-tuple-element.54), channel_id=1, source_target_pairs={{1,0},{2,1},{3,2},{4,3},{5,4},{6,5},{7,6},{0,7},{9,8},{10,9},{11,1... | collective-permute-start | bytes 331784 | tf_op jit(solution)/shard_map/ppermute | solution.py:22
  185.1 15.6 %collective-permute-start.5 = (bf16[12,3,8,192]{3,2,1,0:T(8,128)(2,1)}, bf16[12,3,8,192]{3,2,1,0:T(8,128)(2,1)}, u32[]{:S(2)}, u32[]{:S(2)}) collective-permute-start(bf16[12,3,8,192]{3,2,1,0:T(8,128)(2,1)} %get-tuple-element.48), channel_id=1, source_target_pairs={{1,0},{2,1},{3,2},{4,3},{5,4},{6,5},{7,6},{0,7},{9,8},{10,9},{11,1... | collective-permute-start | bytes 331784 | tf_op jit(solution)/shard_map/ppermute | solution.py:22
  186.6 13.6 %copy-start.8 = (f32[576,192]{0,1:T(8,128)}, f32[576,192]{0,1:T(8,128)S(1)}, u32[]{:S(2)}) copy-start(f32[576,192]{0,1:T(8,128)S(1)} %copy.71) | copy-start | bytes 1327108
  194.5 5.1 copy-start.36
  200.5 10.6 %copy-start.5 = (f32[576,192]{0,1:T(8,128)}, f32[576,192]{0,1:T(8,128)S(1)}, u32[]{:S(2)}) copy-start(f32[576,192]{0,1:T(8,128)S(1)} %get-tuple-element.62) | copy-start | bytes 1327108
  202.8 5.6 copy-start.39
  203.0 5.4 copy-start.57
  215.0 6.3 copy-start.3
  229.0 5.9 copy-start.4
  242.3 4.4 copy-start.9
  242.9 5.1 copy-start.32
  244.4 4.5 copy-start.38
  244.4 4.5 copy-start.40
  246.7 4.7 copy-start.28
  366.3 268.1 %all-reduce.21.cloned.1.call-start = ((), (), s32[]{:S(2)}) async-start(), calls=%async_computation.1 | async-start | bytes 3735552 | tf_op jit(solution)/shard_map/psum | solution.py:194
  368.9 8.1 %collective-permute-start.6 = (bf16[12,3,8,192]{3,2,1,0:T(8,128)(2,1)S(1)}, bf16[12,3,8,192]{3,2,1,0:T(8,128)(2,1)S(1)}, u32[]{:S(2)}, u32[]{:S(2)}) collective-permute-start(bf16[12,3,8,192]{3,2,1,0:T(8,128)(2,1)S(1)} %fusion.48), channel_id=1, source_target_pairs={{7,0},{0,1},{1,2},{2,3},{3,4},{4,5},{5,6},{6,7},{15,8},{8,9},{9,10... | collective-permute-start | bytes 331784 | tf_op jit(solution)/shard_map/ppermute | solution.py:22
  371.8 9.4 %collective-permute-start.2 = (bf16[12,3,8,192]{3,2,1,0:T(8,128)(2,1)S(1)}, bf16[12,3,8,192]{3,2,1,0:T(8,128)(2,1)S(1)}, u32[]{:S(2)}, u32[]{:S(2)}) collective-permute-start(bf16[12,3,8,192]{3,2,1,0:T(8,128)(2,1)S(1)} %fusion.50), channel_id=1, source_target_pairs={{7,0},{0,1},{1,2},{2,3},{3,4},{4,5},{5,6},{6,7},{15,8},{8,9},{9,10... | collective-permute-start | bytes 331784 | tf_op jit(solution)/shard_map/ppermute | solution.py:22
  377.2 98.6 %collective-permute-start.7 = (bf16[6,6,8,192]{3,2,1,0:T(8,128)(2,1)S(1)}, bf16[6,6,8,192]{3,2,1,0:T(8,128)(2,1)S(1)}, u32[]{:S(2)}, u32[]{:S(2)}) collective-permute-start(bf16[6,6,8,192]{3,2,1,0:T(8,128)(2,1)S(1)} %get-tuple-element.45), channel_id=1, source_target_pairs={{120,0},{0,8},{8,16},{16,24},{24,32},{32,40},{40,48},{48,56},{56,6... | collective-permute-start | bytes 331784 | tf_op jit(solution)/shard_map/ppermute | solution.py:22
  381.3 95.3 %collective-permute-start.3 = (bf16[6,6,8,192]{3,2,1,0:T(8,128)(2,1)S(1)}, bf16[6,6,8,192]{3,2,1,0:T(8,128)(2,1)S(1)}, u32[]{:S(2)}, u32[]{:S(2)}) collective-permute-start(bf16[6,6,8,192]{3,2,1,0:T(8,128)(2,1)S(1)} %get-tuple-element.51), channel_id=1, source_target_pairs={{120,0},{0,8},{8,16},{16,24},{24,32},{32,40},{40,48},{48,56},{56,6... | collective-permute-start | bytes 331784 | tf_op jit(solution)/shard_map/ppermute | solution.py:22
  475.8 164.9 %copy-start.1 = (bf16[192,768]{1,0:T(8,128)(2,1)S(1)}, bf16[192,768]{1,0:T(8,128)(2,1)}, u32[]{:S(2)}) copy-start(bf16[192,768]{1,0:T(8,128)(2,1)} %param.10) | copy-start | bytes 884740
  634.4 5.4 copy-start.53
  (39 other events, 96.0 us)
Sparse Core Ops, SparseCore 0:
  366.5 107.6 all-reduce.18
  481.1 153.2 all-reduce.20
where the time goes:
time: 657 us; the launch traced here: 648 us
  local copies, waits for them, and re-layouts  301 us (46%)
  waiting for transfers between devices  257 us (39%)
  other arithmetic  31.1 us (5%)
  matrix products  27.2 us (4%)
  starting transfers between devices  16.5 us (3%)
  between operations  15.3 us (2%)
    psum x1, waiting for transfers between devices, per_device(): summed = lax.psum((grads[0], grads[1], grads[2], grads[3]), ('lon', 'lat'))  157 us
    rev x24, local copies, waits for them, and re-layouts, expand_bias(): shaped[..., offset:offset + WLON][..., ::-1]  115 us
    psum x1, waiting for transfers between devices, per_device(): lax.psum(grad_bias.astype(jnp.bfloat16), 'lon').astype(jnp.float32)  92.8 us
    reshape x2, local copies, waits for them, and re-layouts, forward_block(): scores = scores + bias[:, :, None] + probe_scores  63.2 us
    unnamed x137, local copies, waits for them, and re-layouts  35.2 us
    another operation x2, local copies, waits for them, and re-layouts, expand_bias(): jnp.stack([shaped[..., offset:offset + WLON][..., ::-1] for offset in ran...  20.8 us
    reshape x1, local copies, waits for them, and re-layouts, expand_bias(): return stacked.reshape(lat_win, lev_win, head_count, window_len, window_len)  18.4 us
    ppermute x8, starting transfers between devices, passed_along(): return lax.ppermute(block, axis, route)  16.4 us
  transfers between devices with their start and end apart: 10, of which 4 were waited for; matrix products, arithmetic and copies ran while one was open for 29% of the time, Pallas kernels for 0%

commit v1 on v0

v1 whole, which is shorter than its diff:
```python
import functools
import math

import jax
import jax.numpy as jnp
import numpy as np
from jax import lax
from jax.experimental import pallas as pl
from jax.experimental.pallas import tpu as pltpu
from jax.sharding import PartitionSpec as P

C = 192
HEADS = 6
HIDDEN = 768
LEV = 8
WLON = 12
WLAT = 6
WLEV = 2
LWIN = LEV // WLEV
WH = LWIN * HEADS
WIN = WLEV * WLAT * WLON
TOK = LWIN * WIN
QUAD = TOK // 4
SITE = WLEV * WLAT
SHIFTS = 2 * WLON - 1
STRIP = SHIFTS * SITE
POS = WLEV * WLEV * WLAT * WLAT * SHIFTS
RUN = WLAT * SHIFTS
LANES = 384
STACK = HEADS * WIN
EPSILON = 1e-05
MASKED = -1000000000.0
LOG2E = math.log2(math.e)
SCALE = 1.0 / math.sqrt(C // HEADS)
RING = 4
E_TILES = 72
L_TILES = 36
B_TILES = 27
B_ROOM = 32
PACKED = 224
TILE = (16, 128)
BF16 = jnp.bfloat16
F32 = jnp.float32
MESH = pl.DeviceIdType.MESH
VMEM_LIMIT = 30 * 1024 * 1024


def token_places():
    w, o, lev, a = np.meshgrid(
        np.arange(LWIN), np.arange(WLON), np.arange(WLEV), np.arange(WLAT), indexing="ij"
    )
    quarter = (o // 6) * 2 + a // 3
    level = (2 * w + lev + 1) % LEV
    return (quarter * QUAD + ((o % 6) * 3 + a % 3) * LEV + level).reshape(TOK).astype(np.int32)


def lane_places():
    lev, a, d = np.meshgrid(np.arange(WLEV), np.arange(WLAT), np.arange(SHIFTS), indexing="ij")
    return ((SHIFTS - 1 - d) * SITE + lev * WLAT + a).reshape(STRIP).astype(np.int32)


def row_places():
    wh, _, site = np.meshgrid(np.arange(WH), np.arange(2), np.arange(SITE), indexing="ij")
    return (site * WH + wh).reshape(WH * 2 * SITE).astype(np.int32)


def row_codes():
    _, w, p, lev, a = np.meshgrid(
        np.arange(HEADS), np.arange(LWIN), np.arange(2), np.arange(WLEV), np.arange(WLAT), indexing="ij"
    )
    code = lev + 2 * (a >= WLAT // 2) + 4 * (w == LWIN - 1) + 8 * (p == 0)
    return code.reshape(WH * 2 * SITE).astype(np.int32)


def lane_codes():
    site = np.arange(LANES) % SITE
    return (site // WLAT + 2 * (site % WLAT >= WLAT // 2)).astype(np.int32)


def columns_of(*arrays):
    made = np.zeros((TOK, 8), np.int32)
    for i, array in enumerate(arrays):
        made[: len(array), i] = array
    return made


def dot(a, b):
    return jnp.dot(a, b, preferred_element_type=F32)


def dot_nt(a, b):
    return lax.dot_general(a, b, (((1,), (1,)), ((), ())), preferred_element_type=F32)


def dot_tn(a, b):
    return lax.dot_general(a, b, (((0,), (0,)), ((), ())), preferred_element_type=F32)


def one_hot(places, rows, cols):
    along = 1 if places.shape[1] == 1 else 0
    index = lax.broadcasted_iota(jnp.int32, (rows, cols), along)
    return jnp.where(index == places, 1.0, 0.0).astype(BF16)


def pieces(value, count):
    found = []
    for _ in range(count):
        part = value.astype(BF16)
        found.append(part)
        value = value - part.astype(F32)
    return found


def quarter(ref, index):
    part = ref[pl.ds((index // 2) * 6, 6), pl.ds((index % 2) * 3, 3)]
    return part.astype(F32).reshape(QUAD, C)


def pack(value):
    half = QUAD // 2
    rest = jnp.concatenate([value[:half, 128:], value[half:, 128:]], axis=1)
    blank = jnp.zeros((PACKED - QUAD - half, 128), F32)
    return jnp.concatenate([value[:, :128], rest, blank], axis=0).astype(BF16)


def unpack(value):
    half = QUAD // 2
    wide = value.astype(F32)
    rest = wide[QUAD : QUAD + half]
    right = jnp.concatenate([rest[:, :64], rest[:, 64:]], axis=0)
    return jnp.concatenate([wide[:QUAD], right], axis=1)


def place_of(lon, lat):
    x = lax.rem(lat, 2) * 2 + lax.div(lon, 8)
    return (x, lax.rem(lax.div(lon, 2), RING), lax.div(lat, 2)), lax.rem(lon, 2)


def device_at(chip, core):
    x, y, z = chip
    return ((lax.rem(x, 2) * RING + y) * 2 + core, z * 2 + lax.div(x, 2))


def moved(chip, axis, step):
    return tuple(lax.rem(c + step, RING) if i == axis else c for i, c in enumerate(chip))


def remote(src, dst, send, recv, device):
    return pltpu.make_async_remote_copy(
        src_ref=src, dst_ref=dst, send_sem=send, recv_sem=recv, device_id=device, device_id_type=MESH
    )


class Here:
    def __init__(self, n_lon, n_lat):
        self.lon, self.lat = lax.axis_index("lon"), lax.axis_index("lat")
        self.chip, self.core = place_of(self.lon, self.lat)
        self.sibling = (self.lon + 1 - 2 * self.core, self.lat)
        self.slot = [[lax.rem(c + k, RING) for k in range(RING)] for c in self.chip]
        self.along = [
            [device_at(moved(self.chip, axis, k), self.core) for k in range(RING)] for axis in range(3)
        ]
        self.eighth = lax.div(self.lon, 2)
        self.eighths = [lax.rem(self.eighth + k, 8) for k in range(8)]
        self.rows = [(chip * 2 + self.core, self.lat) for chip in self.eighths]
        self.across = {}
        for step in (-1, 1):
            to_lon = lax.rem(self.lon + n_lon + step, n_lon)
            to_lat = lax.rem(self.lat + n_lat + step, n_lat)
            self.across[step] = ((to_lon, to_lat), (to_lon, self.lat), (self.lon, to_lat))

    def greet(self):
        others = [*self.across[-1], *self.across[1], *self.rows[1:], self.sibling]
        for axis in range(3):
            others += self.along[axis][1:]
        barrier = pltpu.get_barrier_semaphore()
        for device in others:
            pl.semaphore_signal(barrier, inc=1, device_id=device, device_id_type=MESH)
        return lambda: pl.semaphore_wait(barrier, len(others))


def halo(here, source, target, send, recv, step):
    copies = []
    for index in range(3):
        src = index if step < 0 else 3 - index
        device = here.across[step][index]
        copies.append(remote(source.at[src], target.at[3 - src], send.at[index], recv.at[index], device))
    return copies


def begin(copies):
    for copy in copies:
        copy.start()


def end(copies):
    for copy in copies:
        copy.wait()


def wait_bytes(like, sem):
    pltpu.make_async_copy(like, like, sem).wait()


class WeightSum:
    def __init__(self, here, out, refs):
        self.here, self.out = here, out
        self.src, self.other, self.a1, self.r1, self.x2, self.x3, self.send, self.recv = refs

    @staticmethod
    def scratch(tiles):
        n1 = tiles // 12
        room = lambda *dims: pltpu.VMEM((*dims, *TILE), BF16)
        dma = pltpu.SemaphoreType.DMA
        return [
            room(2, tiles), room(tiles),
            room(3, RING, n1), room(3, RING - 1, n1), room(3, RING, n1), room(3, RING, n1),
            dma((6,)), dma((6,)),
        ]

    def put(self, half, block, first=0):
        narrow = block.astype(BF16)
        for c in range(block.shape[1] // 128):
            for r in range(C // 16):
                self.src[half, first + c * 12 + r] = narrow[
                    r * 16 : (r + 1) * 16, c * 128 : (c + 1) * 128
                ]

    def copies(self, at, axis_of, source, target):
        made = []
        for t in range(3):
            axis = (t + axis_of) % 3
            slot = self.here.slot[axis]
            for k in range(1, RING):
                made.append(
                    remote(
                        source(t, slot[k], slot[0]), target(t, k - 1, slot[0]),
                        self.send.at[at], self.recv.at[at], self.here.along[axis][k],
                    )
                )
        return made

    def phase(self, at):
        core = self.here.core
        if at == 0:
            return [remote(self.src.at[1 - core], self.other, self.send.at[0], self.recv.at[0], self.here.sibling)]
        if at == 1:
            return self.copies(1, 0, lambda t, to, me: self.a1.at[t, to], lambda t, k, me: self.r1.at[t, k])
        if at == 2:
            return self.copies(2, 1, lambda t, to, me: self.x2.at[t, me], lambda t, k, me: self.x2.at[t, me])
        if at == 3:
            return self.copies(3, 2, lambda t, to, me: self.x3.at[t, me], lambda t, k, me: self.x3.at[t, me])
        if at == 4:
            out = self.out.at[core]
            return self.copies(4, 0, lambda t, to, me: out.at[t, me], lambda t, k, me: out.at[t, me])
        return [remote(self.out.at[core], self.out.at[core], self.send.at[5], self.recv.at[5], self.here.sibling)]

    def start(self):
        begin(self.phase(0))

    def step(self, at):
        like = self.other if at in (0, 5) else self.r1
        wait_bytes(like, self.recv.at[at])
        wait_bytes(like, self.send.at[at])
        core = self.here.core
        if at == 0:
            total = self.src[core].astype(F32) + self.other[...].astype(F32)
            self.a1[...] = total.astype(BF16).reshape(self.a1.shape)
        for t in range(3):
            one, two, three = (self.here.slot[(t + i) % 3][0] for i in range(3))
            if at == 1:
                total = self.a1[t, one].astype(F32)
                for k in range(RING - 1):
                    total = total + self.r1[t, k].astype(F32)
                self.x2[t, two] = total.astype(BF16)
            if at in (2, 3):
                came = self.x2 if at == 2 else self.x3
                total = came[t, 0].astype(F32)
                for k in range(1, RING):
                    total = total + came[t, k].astype(F32)
                if at == 2:
                    self.x3[t, three] = total.astype(BF16)
                else:
                    self.out[core, t, one] = total.astype(BF16)
        if at < 5:
            begin(self.phase(at + 1))


class BiasSum:
    def __init__(self, here, out, refs):
        self.here, self.out = here, out
        self.src, self.other, self.a1, self.r1, self.send, self.recv = refs

    @staticmethod
    def scratch():
        room = lambda *dims: pltpu.VMEM((*dims, *TILE), BF16)
        dma = pltpu.SemaphoreType.DMA
        return [room(2, B_ROOM), room(B_ROOM), room(8, 4), room(7, 4), dma((4,)), dma((4,))]

    def put(self, block):
        narrow = block.astype(BF16)
        for c in range(3):
            for r in range(18):
                t = c * 18 + r
                self.src[t // B_TILES, t % B_TILES] = narrow[
                    r * 16 : (r + 1) * 16, c * 128 : (c + 1) * 128
                ]
        self.src[0, B_TILES:] = jnp.zeros((B_ROOM - B_TILES, *TILE), BF16)
        self.src[1, B_TILES:] = jnp.zeros((B_ROOM - B_TILES, *TILE), BF16)

    def phase(self, at):
        here, core = self.here, self.here.core
        sems = self.send.at[at], self.recv.at[at]
        if at == 0:
            return [remote(self.src.at[1 - core], self.other, *sems, here.sibling)]
        if at == 3:
            return [remote(self.out.at[core], self.out.at[core], *sems, here.sibling)]
        made = []
        for k in range(1, 8):
            source = self.a1.at[here.eighths[k]] if at == 1 else self.out.at[core, here.eighth]
            target = self.r1.at[k - 1] if at == 1 else self.out.at[core, here.eighth]
            made.append(remote(source, target, *sems, here.rows[k]))
        return made

    def start(self):
        begin(self.phase(0))

    def step(self, at):
        like = (self.other, self.r1, self.r1, self.other)[at]
        wait_bytes(like, self.recv.at[at])
        wait_bytes(like, self.send.at[at])
        core, chip = self.here.core, self.here.eighth
        if at == 0:
            total = self.src[core].astype(F32) + self.other[...].astype(F32)
            self.a1[...] = total.astype(BF16).reshape(8, 4, *TILE)
        if at == 1:
            total = self.a1[chip].astype(F32)
            for k in range(7):
                total = total + self.r1[k].astype(F32)
            self.out[core, chip] = total.astype(BF16)
        if at < 3:
            begin(self.phase(at + 1))


def layer_norm(x):
    centered = x - jnp.mean(x, axis=-1, keepdims=True)
    spread = jnp.mean(centered * centered, axis=-1, keepdims=True)
    rate = lax.rsqrt(spread + EPSILON)
    return centered * rate, rate


def layer_norm_back(cot, unit, rate):
    first = jnp.mean(cot, axis=-1, keepdims=True)
    second = jnp.mean(cot * unit, axis=-1, keepdims=True)
    return rate * (cot - first - unit * second)


def head_mask(head):
    lane = lax.broadcasted_iota(jnp.int32, (1, C), 1)
    return (lane >= head * 32) & (lane < head * 32 + 32)


def stacked(value):
    wide = value.astype(F32)
    parts = [jnp.where(head_mask(h), wide, 0.0).astype(BF16) for h in range(HEADS)]
    return jnp.concatenate(parts, axis=0)


def unstacked(value):
    total = jnp.where(head_mask(0), value[0:WIN], 0.0)
    for h in range(1, HEADS):
        total = total + jnp.where(head_mask(h), value[h * WIN : (h + 1) * WIN], 0.0)
    return total


def expand_bias(last_lat, table, columns, index_rows, lanes, tall_table, gathered, strips, scores):
    for head in range(HEADS):
        tall_table[head * LWIN : (head + 1) * LWIN, :] = table[head]
    for site in range(SITE):
        lev, a = site // WLAT, site % WLAT
        for other in range(WLEV):
            start = ((lev * WLEV + other) * WLAT + a) * RUN
            gathered[site * WH : (site + 1) * WH, other * RUN : (other + 1) * RUN] = tall_table[
                :, start : start + RUN
            ]
    moved = sum(dot(part, lanes[...]) for part in pieces(gathered[...], 3))
    rows = one_hot(columns[:, 1:2], WH * 2 * SITE, SITE * WH)
    moved = sum(dot(rows, part) for part in pieces(moved, 3))
    code = columns[:, 2:3]
    moved = jnp.where((code & 8) != 0, pltpu.roll(moved, LANES - SITE, 1), moved) * LOG2E
    seen = jnp.where((code & 4) != 0, 1, 0) + jnp.where(last_lat, 2, 0)
    apart = (code ^ index_rows[2:3, 0:LANES]) & seen
    strips[...] = jnp.where(apart != 0, MASKED, moved)

    def one(wh, carry):
        strip = strips[pl.ds(pl.multiple_of(wh * 2 * SITE, 8), 2 * SITE), :]
        start = lax.rem(wh, LWIN) * STACK + lax.div(wh, LWIN) * WIN
        for pair in range(WLON // 2):
            offset = (WLON - 2 - 2 * pair) * SITE
            scores[pl.ds(pl.multiple_of(start + pair * 24, 8), 24), :] = strip[
                :, offset : offset + WIN
            ]
        return carry

    lax.fori_loop(0, WH, one, 0)


def collapse_bias(first, last, scores, strips):
    def one(wh, carry):
        start = lax.rem(wh, LWIN) * STACK + lax.div(wh, LWIN) * WIN
        total = jnp.zeros((2 * SITE, LANES), F32)
        for pair in range(WLON // 2):
            offset = (WLON - 2 - 2 * pair) * SITE
            part = scores[pl.ds(pl.multiple_of(start + pair * 24, 8), 24), :]
            part = jnp.concatenate([part, jnp.zeros((2 * SITE, LANES - WIN), F32)], axis=1)
            total = total + (pltpu.roll(part, offset, 1) if offset else part)
        strips[pl.ds(pl.multiple_of(wh * 2 * SITE, 8), 2 * SITE), :] = total
        return carry

    lax.fori_loop(first, last, one, 0)


def join_strips(strips, columns, index_rows):
    total = strips[...]
    total = jnp.where((columns[:, 2:3] & 8) != 0, pltpu.roll(total, SITE, 1), total)
    rows = one_hot(index_rows[1:2, :], SITE * WH, WH * 2 * SITE)
    return sum(dot(rows, part) for part in pieces(total, 2))


def block_kernel(n_lon, n_lat, *refs):
    loaded = refs[:9]
    out_field, grad_field, qkv, proj, fc1, fc2, bias = refs[9:16]
    field, cot, w_qkv, w_proj, w_fc1, w_fc2, table, columns, index_rows, load_sem = refs[16:26]
    (
        out, e_out, l_out, b_out, sent, came, back, halo_send, halo_recv,
        xw, uw, scores, normed, query, key, value, unit, rate, blended, normed_two, hidden,
        cot_first, cot_mid, cot_q, cot_k, cot_v, ow, gw, tall_table, gathered, strips, w3,
        places_in, places_out, lanes,
    ) = refs[26:61]
    here = Here(n_lon, n_lat)
    early = WeightSum(here, e_out, refs[61:69])
    late = WeightSum(here, l_out, refs[69:77])
    strip_sum = BiasSum(here, b_out, refs[77:83])

    loads = [
        pltpu.make_async_copy(src, dst, load_sem.at[i]) for i, (src, dst) in enumerate(zip(loaded, refs[16:25]))
    ]
    begin(loads)
    greeted = here.greet()
    loads[0].wait()
    for index in range(3):
        sent[0, index] = pack(quarter(field, index))
    greeted()
    inward = [
        halo(here, sent.at[i], came.at[i], halo_send.at[i], halo_recv.at[i], -1) for i in range(2)
    ]
    outward = [
        halo(here, back.at[i], out.at[i], halo_send.at[2 + i], halo_recv.at[2 + i], 1) for i in range(2)
    ]
    begin(inward[0])
    end(loads[6:9])
    lanes[...] = one_hot(columns[0:STRIP, 3:4], STRIP, LANES)
    last_lat = here.lat == n_lat - 1
    expand_bias(last_lat, table, columns, index_rows, lanes, tall_table, gathered, strips, scores)
    places_in[...] = one_hot(columns[:, 0:1], TOK, TOK)
    places_out[...] = one_hot(index_rows[0:1, :], TOK, TOK)
    loads[1].wait()
    for index in range(3):
        sent[1, index] = pack(quarter(cot, index))
    loads[2].wait()
    for third in range(3):
        w3[third] = w_qkv[:, third * C : (third + 1) * C]

    def gather(kind, ref):
        parts = [quarter(ref, 3)] + [unpack(came[kind, i]) for i in range(1, 4)]
        whole = jnp.concatenate(parts, axis=0).astype(BF16)
        return dot(places_in[...], whole).astype(BF16)

    def scatter(kind, ref):
        whole = dot(places_out[...], ref[...])
        out[kind, 3] = pack(whole[:QUAD])
        for i in range(1, 4):
            back[kind, i] = pack(whole[i * QUAD : (i + 1) * QUAD])
        begin(outward[kind])

    def places(w):
        return pl.ds(w * WIN, WIN), pl.ds(w * STACK, STACK)

    def attend(w):
        rows, tall = places(w)
        unit_x, rate_x = layer_norm(xw[rows, :].astype(F32))
        unit[rows, :] = unit_x
        rate[rows, :] = rate_x
        norm = unit_x.astype(BF16)
        normed[rows, :] = norm
        q = dot(norm, w3[0]).astype(BF16)
        k = dot(norm, w3[1]).astype(BF16)
        v = dot(norm, w3[2]).astype(BF16)
        query[rows, :] = q
        key[rows, :] = k
        value[rows, :] = v
        s = dot_nt(stacked(q), k) * (SCALE * LOG2E) + scores[tall, :]
        e = jnp.exp2(s - jnp.max(s, axis=-1, keepdims=True))
        p = e * (1.0 / jnp.sum(e, axis=-1, keepdims=True))
        scores[tall, :] = p
        blended[rows, :] = unstacked(dot(p.astype(BF16), v)).astype(BF16)

    def feed(w):
        rows = pl.ds(w * 2 * WIN, 2 * WIN)
        middle = xw[rows, :].astype(F32) + dot(blended[rows, :], w_proj[...])
        middle = middle.astype(BF16).astype(F32)
        unit_m, rate_m = layer_norm(middle)
        norm_m = unit_m.astype(BF16)
        normed_two[rows, :] = norm_m
        first = dot(norm_m, w_fc1[...])
        phi = 0.5 + 0.5 * lax.erf(first * math.sqrt(0.5))
        hid = (first * phi).astype(BF16)
        hidden[rows, :] = hid
        bell = jnp.exp2(first * first * (-0.5 * LOG2E)) * (1.0 / math.sqrt(2.0 * math.pi))
        slope = phi + first * bell
        ow[rows, :] = (middle + dot_nt(hid, w_fc2[...])).astype(BF16)
        up = uw[rows, :]
        c_first = (dot(up, w_fc2[...]).astype(BF16).astype(F32) * slope).astype(BF16)
        cot_first[rows, :] = c_first
        c_norm = dot_nt(c_first, w_fc1[...]).astype(BF16).astype(F32)
        c_mid = layer_norm_back(c_norm, unit_m, rate_m).astype(BF16).astype(F32)
        cot_mid[rows, :] = (up.astype(F32) + c_mid).astype(BF16)

    def backward(w):
        rows, tall = places(w)
        up = cot_mid[rows, :]
        c_blend = stacked(dot_nt(up, w_proj[...]).astype(BF16))
        p = scores[tall, :]
        c_p = dot_nt(c_blend, value[rows, :])
        c_s = p * (c_p - jnp.sum(p * c_p, axis=-1, keepdims=True))
        scores[tall, :] = c_s
        c_v = dot_tn(p.astype(BF16), c_blend).astype(BF16)
        narrow = c_s.astype(BF16)
        c_q = (unstacked(dot(narrow, key[rows, :])) * SCALE).astype(BF16)
        c_k = (dot_tn(narrow, stacked(query[rows, :])) * SCALE).astype(BF16)
        cot_q[rows, :] = c_q
        cot_k[rows, :] = c_k
        cot_v[rows, :] = c_v

    def inputs_back(w):
        rows = pl.ds(w * 2 * WIN, 2 * WIN)
        c_norm = dot_nt(cot_q[rows, :], w3[0]) + dot_nt(cot_k[rows, :], w3[1])
        c_norm = (c_norm + dot_nt(cot_v[rows, :], w3[2])).astype(BF16).astype(F32)
        c_x = layer_norm_back(c_norm, unit[rows, :], rate[rows, :]).astype(BF16)
        gw[rows, :] = (cot_mid[rows, :].astype(F32) + c_x.astype(F32)).astype(BF16)

    end(inward[0])
    begin(inward[1])
    xw[...] = gather(0, field)
    for w in range(LWIN):
        attend(w)
    end(loads[3:6])
    end(inward[1])
    uw[...] = gather(1, cot)
    feed(0)
    feed(1)
    early.put(0, dot_tn(normed_two[...], cot_first[...]))
    early.put(1, dot_tn(uw[...], hidden[...]))
    early.start()
    scatter(0, ow)
    backward(0)
    backward(1)
    early.step(0)
    backward(2)
    backward(3)
    early.step(1)
    norm = normed[...]
    late.put(0, jnp.concatenate([dot_tn(norm, cot_q[...]), dot_tn(norm, cot_k[...])], axis=1))
    c_proj = dot_tn(blended[...], cot_mid[...])
    late.put(1, jnp.concatenate([dot_tn(norm, cot_v[...]), c_proj], axis=1))
    late.start()
    collapse_bias(0, WH, scores, strips)
    strip_sum.put(join_strips(strips, columns, index_rows))
    strip_sum.start()
    late.step(0)
    early.step(2)
    strip_sum.step(0)
    late.step(1)
    early.step(3)
    inputs_back(0)
    inputs_back(1)
    scatter(1, gw)
    late.step(2)
    early.step(4)
    late.step(3)
    strip_sum.step(1)
    end(outward[0])
    for index in range(4):
        whole_quarter(out_field, index, out[0, index])
    early.step(5)
    fc1[...] = joined(tiles_of(e_out, 0), 6)
    fc2[...] = joined(tiles_of(e_out, 1), 6)
    late.step(4)
    strip_sum.step(2)
    end(outward[1])
    for index in range(4):
        whole_quarter(grad_field, index, out[1, index])
    late.step(5)
    qkv[:, 0:384] = joined(tiles_of(l_out, 0), 3)
    right = joined(tiles_of(l_out, 1), 3)
    qkv[:, 384:576] = right[:, 0:C]
    proj[...] = right[:, C:]
    strip_sum.step(3)
    finish_bias(b_out, lanes, tall_table, bias)


def whole_quarter(target, index, packed):
    part = unpack(packed).reshape(6, 3, LEV, C).astype(BF16)
    target[pl.ds((index // 2) * 6, 6), pl.ds((index % 2) * 3, 3)] = part


def joined(tiles, columns):
    rows = len(tiles) // columns
    cols = [jnp.concatenate(tiles[c * rows : (c + 1) * rows], axis=0) for c in range(columns)]
    return jnp.concatenate(cols, axis=1).astype(F32)


def tiles_of(ref, half):
    n1 = ref.shape[3]
    return [ref[half, i // (4 * n1), i // n1 % 4, i % n1] for i in range(12 * n1)]


def finish_bias(b_in, lanes, tall_table, bias):
    tiles = [b_in[t // B_TILES, t % B_TILES // 4, t % B_TILES % 4] for t in range(2 * B_TILES)]
    runs = dot_nt(joined(tiles, 3).astype(BF16), lanes[...])
    for site in range(SITE):
        lev, a = site // WLAT, site % WLAT
        for other in range(WLEV):
            start = ((lev * WLEV + other) * WLAT + a) * RUN
            tall_table[:, start : start + RUN] = runs[
                site * WH : (site + 1) * WH, other * RUN : (other + 1) * RUN
            ]
    for head in range(HEADS):
        bias[head] = tall_table[head * LWIN : (head + 1) * LWIN, :]


def finish_kernel(*refs):
    count = len(refs) // 2
    copies = [pltpu.make_async_copy(refs[i], refs[count + i], refs[-1].at[i]) for i in range(count)]
    begin(copies)
    end(copies)


def per_device(n_lon, n_lat, field, w_qkv, w_proj, w_fc1, w_fc2, bias_table, cotangent):
    vmem, hbm = pl.BlockSpec(memory_space=pltpu.VMEM), pl.BlockSpec(memory_space=pltpu.HBM)
    shape = jax.ShapeDtypeStruct
    dma = pltpu.SemaphoreType.DMA
    rows = row_places()
    columns = columns_of(token_places(), rows, row_codes(), lane_places())
    index_rows = columns_of(token_places(), rows, lane_codes()).T.copy()
    inputs = (
        field, cotangent, w_qkv, w_proj, w_fc1, w_fc2.T, bias_table[0].transpose(1, 0, 2), columns, index_rows
    )
    inputs = [pltpu.with_memory_space_constraint(jnp.asarray(a), pltpu.HBM) for a in inputs]
    tile = shape((WLON, WLAT, LEV, C), BF16)
    outputs = (
        tile,
        tile,
        shape((C, 3 * C), F32),
        shape((C, C), F32),
        shape((C, HIDDEN), F32),
        shape((C, HIDDEN), F32),
        shape((HEADS, LWIN, POS), F32),
    )
    wide = lambda dtype, n=1: [pltpu.VMEM((TOK, C), dtype)] * n
    results = pl.pallas_call(
        functools.partial(block_kernel, n_lon, n_lat),
        out_shape=outputs,
        in_specs=[hbm] * len(inputs),
        out_specs=[vmem] * len(outputs),
        scratch_shapes=[
            *[pltpu.VMEM(a.shape, a.dtype) for a in inputs],
            dma((len(inputs),)),
            pltpu.VMEM((2, 4, PACKED, 128), BF16),
            pltpu.VMEM((2, 3, RING, E_TILES // 12, *TILE), BF16),
            pltpu.VMEM((2, 3, RING, L_TILES // 12, *TILE), BF16),
            pltpu.VMEM((2, 8, B_ROOM // 8, *TILE), BF16),
            pltpu.VMEM((2, 3, PACKED, 128), BF16),
            pltpu.VMEM((2, 4, PACKED, 128), BF16),
            pltpu.VMEM((2, 4, PACKED, 128), BF16),
            dma((4, 3)),
            dma((4, 3)),
            *wide(BF16, 2),
            pltpu.VMEM((LWIN * STACK, WIN), F32),
            *wide(BF16, 4),
            *wide(F32),
            pltpu.VMEM((TOK, 1), F32),
            *wide(BF16, 2),
            pltpu.VMEM((TOK, HIDDEN), BF16),
            pltpu.VMEM((TOK, HIDDEN), BF16),
            *wide(BF16, 6),
            pltpu.VMEM((WH, POS), F32),
            pltpu.VMEM((SITE * WH, STRIP), F32),
            pltpu.VMEM((WH * 2 * SITE, LANES), F32),
            pltpu.VMEM((3, C, C), BF16),
            pltpu.VMEM((TOK, TOK), BF16),
            pltpu.VMEM((TOK, TOK), BF16),
            pltpu.VMEM((STRIP, LANES), BF16),
            *WeightSum.scratch(E_TILES),
            *WeightSum.scratch(L_TILES),
            *BiasSum.scratch(),
        ],
        compiler_params=pltpu.CompilerParams(
            vmem_limit_bytes=VMEM_LIMIT, collective_id=0, has_side_effects=True
        ),
        name="block",
    )(*inputs)
    *results, fc2, bias = pl.pallas_call(
        finish_kernel,
        out_shape=outputs,
        in_specs=[vmem] * len(outputs),
        out_specs=[hbm] * len(outputs),
        scratch_shapes=[dma((len(outputs),))],
        compiler_params=pltpu.CompilerParams(vmem_limit_bytes=VMEM_LIMIT),
        name="finish",
    )(*results)
    return (*results, fc2.T, bias.transpose(1, 0, 2)[None])


def solution(mesh):
    whole, tiles, banded = P(), P("lon", "lat", None, None), P("lat", None, None, None)
    return jax.shard_map(
        functools.partial(per_device, mesh.shape["lon"], mesh.shape["lat"]),
        mesh=mesh,
        in_specs=(tiles, whole, whole, whole, whole, banded, tiles),
        out_specs=(tiles, tiles, whole, whole, whole, whole, banded),
        check_vma=False,
    )
```

time: 657 us -> 55.9 us (0.09); the launches traced: 648 us -> 55.7 us
  local copies, waits for them, and re-layouts: 301 us -> 0 us
  waiting for transfers between devices: 257 us -> 0 us
  Pallas kernels: 0 us -> 54.9 us
  other arithmetic: 31.1 us -> 0 us
  matrix products: 27.2 us -> 0 us
  starting transfers between devices: 16.5 us -> 0 us
  between operations: 15.3 us -> 0.8 us
    psum x2 -> x0, waiting for transfers between devices: 250 us -> none  [the longest x1 157 us: per_device(): summed = lax.psum((grads[0], grads[1], grads[2], grads[3]), ('lon', 'lat'))]
    rev x24 -> x0, local copies, waits for them, and re-layouts: 115 us -> none  [expand_bias(): shaped[..., offset:offset + WLON][..., ::-1]]
    reshape x15 -> x0, local copies, waits for them, and re-layouts: 95.2 us -> none  [the longest x2 63.2 us: forward_block(): scores = scores + bias[:, :, None] + probe_scores]
    pallas_call x0 -> x2, Pallas kernels: none -> 54.9 us  [the longest x1 53.3 us: per_device(): pl.pallas_call(functools.partial(block_kernel, n_lon, n_lat), out_shape=o...]
    unnamed x137 -> x0, local copies, waits for them, and re-layouts: 35.2 us -> none
    dot_general x18 -> x0, matrix products: 27.2 us -> none  [the longest x3 6.81 us: forward_block(): jnp.einsum('avonhd,avomhd->avohnm', queries, key_part, preferred_element_...]
    another operation x3 -> x0, local copies, waits for them, and re-layouts: 24.1 us -> none  [the longest x2 20.8 us: expand_bias(): jnp.stack([shaped[..., offset:offset + WLON][..., ::-1] for offset in ran...]
    slice x11 -> x0, local copies, waits for them, and re-layouts: 16.8 us -> none  [the longest x1 12.8 us: expand_bias(): shaped[..., offset:offset + WLON][..., ::-1]]
  transfers between devices with their start and end apart: 10 -> 0, of which waited for: 4 -> 0; matrix products, arithmetic and copies ran while one was open for 29% -> 0% of each run, Pallas kernels for 0% -> 0%
where the time goes in v1:
time: 55.9 us; the launch traced here: 55.7 us
  Pallas kernels  54.9 us (98%)
  between operations  0.8 us (1%)
    pallas_call x1, Pallas kernels, per_device(): pl.pallas_call(functools.partial(block_kernel, n_lon, n_lat), out_shape=o...  53.3 us
    pallas_call x1, Pallas kernels, per_device(): pl.pallas_call(finish_kernel, out_shape=outputs, in_specs=[vmem] * len(ou...  1.6 us

profile of v1, /device:TPU:1, one launch (start us, length us, event | category | flops | bytes accessed | tf_op | source)
XLA Modules:
  0.0 55.7 jit_solution(9090871944659738526)
XLA Ops:
  0.6 53.3 %block.1 = (bf16[12,6,8,192]{3,2,1,0:T(8,128)(2,1)S(1)}, bf16[12,6,8,192]{3,2,1,0:T(8,128)(2,1)S(1)}, f32[192,576]{1,0:T(8,128)S(1)}, f32[192,192]{1,0:T(8,128)S...) custom-call(bf16[12,6,8,192]{3,2,1,0:T(8,128)(2,1)} %refs_0_.1, ...), custom_call_target="tpu_custom_call" | custom-call | tf_op jit(solution)/shard_map/block/pallas_call | solution.py:671
  54.0 1.6 %finish.1 = (bf16[12,6,8,192]{3,2,1,0:T(8,128)(2,1)}, bf16[12,6,8,192]{3,2,1,0:T(8,128)(2,1)}, f32[192,576]{1,0:T(8,128)}, f32[192,192]{1,0:T(8,128)}, f32[192,7...) custom-call(bf16[12,6,8,192]{3,2,1,0:T(8,128)(2,1)S(1)} %get-tuple-element.21.refs_0_, ...), custom_call_target="tpu_custom_call" | custom-call | tf_op jit(solution)/shard_map/finish/pallas_call | solution.py:713

commit v2 on v1

--- a/solution.py
+++ b/solution.py
@@ -33,10 +33,11 @@
 LOG2E = math.log2(math.e)
 SCALE = 1.0 / math.sqrt(C // HEADS)
 RING = 4
-E_TILES = 72
-L_TILES = 36
-B_TILES = 27
-B_ROOM = 32
+E_TILES = 144
+L_TILES = 72
+B_TILES = 40
+B_LEFT = STRIP - 256
+B_ROWS = 48
 PACKED = 224
 TILE = (16, 128)
 BF16 = jnp.bfloat16
@@ -155,14 +156,19 @@
     def __init__(self, n_lon, n_lat):
         self.lon, self.lat = lax.axis_index("lon"), lax.axis_index("lat")
         self.chip, self.core = place_of(self.lon, self.lat)
-        self.sibling = (self.lon + 1 - 2 * self.core, self.lat)
         self.slot = [[lax.rem(c + k, RING) for k in range(RING)] for c in self.chip]
-        self.along = [
-            [device_at(moved(self.chip, axis, k), self.core) for k in range(RING)] for axis in range(3)
-        ]
-        self.eighth = lax.div(self.lon, 2)
-        self.eighths = [lax.rem(self.eighth + k, 8) for k in range(8)]
-        self.rows = [(chip * 2 + self.core, self.lat) for chip in self.eighths]
+        chips = [[moved(self.chip, axis, k) for k in range(RING)] for axis in range(3)]
+        self.along = [[device_at(chip, self.core) for chip in ring] for ring in chips]
+        other = 1 - self.core
+        self.eight = []
+        for axis in range(3):
+            found = []
+            for k in range(RING):
+                if k:
+                    found.append((self.along[axis][k], self.slot[axis][k], self.core))
+                found.append((device_at(chips[axis][k], other), self.slot[axis][k], other))
+            self.eight.append(found)
+        self.facing = (lax.rem(self.lon + 8, 16), self.lat)
         self.across = {}
         for step in (-1, 1):
             to_lon = lax.rem(self.lon + n_lon + step, n_lon)
@@ -170,9 +176,9 @@
             self.across[step] = ((to_lon, to_lat), (to_lon, self.lat), (self.lon, to_lat))
 
     def greet(self):
-        others = [*self.across[-1], *self.across[1], *self.rows[1:], self.sibling]
+        others = [*self.across[-1], *self.across[1], self.facing]
         for axis in range(3):
-            others += self.along[axis][1:]
+            others += [device for device, _, _ in self.eight[axis]]
         barrier = pltpu.get_barrier_semaphore()
         for device in others:
             pl.semaphore_signal(barrier, inc=1, device_id=device, device_id_type=MESH)
@@ -202,143 +208,134 @@
     pltpu.make_async_copy(like, like, sem).wait()
 
 
+def room(*dims):
+    return pltpu.VMEM((*dims, *TILE), BF16)
+
+
+def tiles_in(block):
+    narrow = block.astype(BF16)
+    for c in range(block.shape[1] // 128):
+        for r in range(block.shape[0] // 16):
+            yield narrow[r * 16 : (r + 1) * 16, c * 128 : (c + 1) * 128]
+
+
+def added(terms):
+    total = terms[0].astype(F32)
+    for term in terms[1:]:
+        total = total + term.astype(F32)
+    return total.astype(BF16)
+
+
 class WeightSum:
     def __init__(self, here, out, refs):
         self.here, self.out = here, out
-        self.src, self.other, self.a1, self.r1, self.x2, self.x3, self.send, self.recv = refs
+        self.src, self.r1, self.x2, self.x3, self.send, self.recv = refs
 
     @staticmethod
     def scratch(tiles):
-        n1 = tiles // 12
-        room = lambda *dims: pltpu.VMEM((*dims, *TILE), BF16)
+        n1 = tiles // 24
         dma = pltpu.SemaphoreType.DMA
-        return [
-            room(2, tiles), room(tiles),
-            room(3, RING, n1), room(3, RING - 1, n1), room(3, RING, n1), room(3, RING, n1),
-            dma((6,)), dma((6,)),
-        ]
-
-    def put(self, half, block, first=0):
-        narrow = block.astype(BF16)
-        for c in range(block.shape[1] // 128):
-            for r in range(C // 16):
-                self.src[half, first + c * 12 + r] = narrow[
-                    r * 16 : (r + 1) * 16, c * 128 : (c + 1) * 128
-                ]
-
-    def copies(self, at, axis_of, source, target):
-        made = []
+        return [room(3, RING, 2, n1), room(7, 3, n1), room(3, RING, n1), room(3, RING, n1), dma((4,)), dma((4,))]
+
+    def put(self, block, first):
+        n1 = self.src.shape[3]
+        for at, tile in enumerate(tiles_in(block), first):
+            self.src[at // (8 * n1), at // (2 * n1) % RING, at // n1 % 2, at % n1] = tile
+
+    def phase(self, at):
+        here, made = self.here, []
+        sems = self.send.at[at], self.recv.at[at]
         for t in range(3):
-            axis = (t + axis_of) % 3
-            slot = self.here.slot[axis]
-            for k in range(1, RING):
-                made.append(
-                    remote(
-                        source(t, slot[k], slot[0]), target(t, k - 1, slot[0]),
-                        self.send.at[at], self.recv.at[at], self.here.along[axis][k],
-                    )
-                )
+            if at in (0, 3):
+                mine = self.out.at[t, here.slot[t][0], here.core]
+                for k, (device, slot, core) in enumerate(here.eight[t]):
+                    if at == 0:
+                        made.append(remote(self.src.at[t, slot, core], self.r1.at[k, t], *sems, device))
+                    else:
+                        made.append(remote(mine, mine, *sems, device))
+            else:
+                axis = (t + at) % 3
+                mine = (self.x2 if at == 1 else self.x3).at[t, here.slot[axis][0]]
+                made += [remote(mine, mine, *sems, here.along[axis][k]) for k in range(1, RING)]
         return made
-
-    def phase(self, at):
-        core = self.here.core
-        if at == 0:
-            return [remote(self.src.at[1 - core], self.other, self.send.at[0], self.recv.at[0], self.here.sibling)]
-        if at == 1:
-            return self.copies(1, 0, lambda t, to, me: self.a1.at[t, to], lambda t, k, me: self.r1.at[t, k])
-        if at == 2:
-            return self.copies(2, 1, lambda t, to, me: self.x2.at[t, me], lambda t, k, me: self.x2.at[t, me])
-        if at == 3:
-            return self.copies(3, 2, lambda t, to, me: self.x3.at[t, me], lambda t, k, me: self.x3.at[t, me])
-        if at == 4:
-            out = self.out.at[core]
-            return self.copies(4, 0, lambda t, to, me: out.at[t, me], lambda t, k, me: out.at[t, me])
-        return [remote(self.out.at[core], self.out.at[core], self.send.at[5], self.recv.at[5], self.here.sibling)]
 
     def start(self):
         begin(self.phase(0))
 
     def step(self, at):
-        like = self.other if at in (0, 5) else self.r1
+        like = self.r1 if at in (0, 3) else self.r1.at[pl.ds(0, 3)]
         wait_bytes(like, self.recv.at[at])
         wait_bytes(like, self.send.at[at])
         core = self.here.core
-        if at == 0:
-            total = self.src[core].astype(F32) + self.other[...].astype(F32)
-            self.a1[...] = total.astype(BF16).reshape(self.a1.shape)
         for t in range(3):
             one, two, three = (self.here.slot[(t + i) % 3][0] for i in range(3))
+            if at == 0:
+                self.x2[t, two] = added([self.src[t, one, core]] + [self.r1[k, t] for k in range(7)])
             if at == 1:
-                total = self.a1[t, one].astype(F32)
-                for k in range(RING - 1):
-                    total = total + self.r1[t, k].astype(F32)
-                self.x2[t, two] = total.astype(BF16)
-            if at in (2, 3):
-                came = self.x2 if at == 2 else self.x3
-                total = came[t, 0].astype(F32)
-                for k in range(1, RING):
-                    total = total + came[t, k].astype(F32)
-                if at == 2:
-                    self.x3[t, three] = total.astype(BF16)
-                else:
-                    self.out[core, t, one] = total.astype(BF16)
-        if at < 5:
+                self.x3[t, three] = added([self.x2[t, k] for k in range(RING)])
+            if at == 2:
+                self.out[t, one, core] = added([self.x3[t, k] for k in range(RING)])
+        if at < 3:
             begin(self.phase(at + 1))
 
 
 class BiasSum:
     def __init__(self, here, out, refs):
         self.here, self.out = here, out
-        self.src, self.other, self.a1, self.r1, self.send, self.recv = refs
+        self.src, self.r1, self.x2, self.send, self.recv = refs
 
     @staticmethod
     def scratch():
-        room = lambda *dims: pltpu.VMEM((*dims, *TILE), BF16)
+        each = B_TILES // 8
         dma = pltpu.SemaphoreType.DMA
-        return [room(2, B_ROOM), room(B_ROOM), room(8, 4), room(7, 4), dma((4,)), dma((4,))]
+        return [room(RING, 2, each), room(7, each), room(2, each), dma((3,)), dma((3,))]
 
     def put(self, block):
-        narrow = block.astype(BF16)
-        for c in range(3):
-            for r in range(18):
-                t = c * 18 + r
-                self.src[t // B_TILES, t % B_TILES] = narrow[
-                    r * 16 : (r + 1) * 16, c * 128 : (c + 1) * 128
-                ]
-        self.src[0, B_TILES:] = jnp.zeros((B_ROOM - B_TILES, *TILE), BF16)
-        self.src[1, B_TILES:] = jnp.zeros((B_ROOM - B_TILES, *TILE), BF16)
+        each = B_TILES // 8
+        last = block[:, 256:]
+        shared = last[0:B_ROWS]
+        for g in range(1, 288 // B_ROWS):
+            shared = shared + pltpu.roll(last[g * B_ROWS : (g + 1) * B_ROWS], g * B_LEFT, 1)
+        tiles = [*tiles_in(block[:, :256]), *tiles_in(shared), jnp.zeros(TILE, BF16)]
+        for at, tile in enumerate(tiles):
+            self.src[at // (2 * each), at // each % 2, at % each] = tile
+
+    def get(self):
+        each = B_TILES // 8
+        tiles = [self.out[at // (2 * each), at // each % 2, at % each] for at in range(B_TILES)]
+        first = joined(tiles[:36], 2)
+        shared = joined(tiles[36:39], 1)
+        last = [shared]
+        for g in range(1, 288 // B_ROWS):
+            last.append(pltpu.roll(shared, 128 - g * B_LEFT, 1))
+        return jnp.concatenate([first, jnp.concatenate(last, axis=0)], axis=1)
 
     def phase(self, at):
-        here, core = self.here, self.here.core
+        here, made = self.here, []
         sems = self.send.at[at], self.recv.at[at]
-        if at == 0:
-            return [remote(self.src.at[1 - core], self.other, *sems, here.sibling)]
-        if at == 3:
-            return [remote(self.out.at[core], self.out.at[core], *sems, here.sibling)]
-        made = []
-        for k in range(1, 8):
-            source = self.a1.at[here.eighths[k]] if at == 1 else self.out.at[core, here.eighth]
-            target = self.r1.at[k - 1] if at == 1 else self.out.at[core, here.eighth]
-            made.append(remote(source, target, *sems, here.rows[k]))
+        if at == 1:
+            return [remote(self.x2.at[0], self.x2.at[1], *sems, here.facing)]
+        mine = self.out.at[here.slot[1][0], here.core]
+        for k, (device, slot, core) in enumerate(here.eight[1]):
+            if at == 0:
+                made.append(remote(self.src.at[slot, core], self.r1.at[k], *sems, device))
+            else:
+                made.append(remote(mine, mine, *sems, device))
         return made
 
     def start(self):
         begin(self.phase(0))
 
     def step(self, at):
-        like = (self.other, self.r1, self.r1, self.other)[at]
+        like = self.x2.at[1] if at == 1 else self.r1
         wait_bytes(like, self.recv.at[at])
         wait_bytes(like, self.send.at[at])
-        core, chip = self.here.core, self.here.eighth
+        slot, core = self.here.slot[1][0], self.here.core
         if at == 0:
-            total = self.src[core].astype(F32) + self.other[...].astype(F32)
-            self.a1[...] = total.astype(BF16).reshape(8, 4, *TILE)
+            self.x2[0] = added([self.src[slot, core]] + [self.r1[k] for k in range(7)])
         if at == 1:
-            total = self.a1[chip].astype(F32)
-            for k in range(7):
-                total = total + self.r1[k].astype(F32)
-            self.out[core, chip] = total.astype(BF16)
-        if at < 3:
+            self.out[slot, core] = added([self.x2[0], self.x2[1]])
+        if at < 2:
             begin(self.phase(at + 1))
 
 
@@ -438,9 +435,9 @@
         places_in, places_out, lanes,
     ) = refs[26:61]
     here = Here(n_lon, n_lat)
-    early = WeightSum(here, e_out, refs[61:69])
-    late = WeightSum(here, l_out, refs[69:77])
-    strip_sum = BiasSum(here, b_out, refs[77:83])
+    early = WeightSum(here, e_out, refs[61:67])
+    late = WeightSum(here, l_out, refs[67:73])
+    strip_sum = BiasSum(here, b_out, refs[73:78])
 
     loads = [
         pltpu.make_async_copy(src, dst, load_sem.at[i]) for i, (src, dst) in enumerate(zip(loaded, refs[16:25]))
@@ -559,8 +556,8 @@
     uw[...] = gather(1, cot)
     feed(0)
     feed(1)
-    early.put(0, dot_tn(normed_two[...], cot_first[...]))
-    early.put(1, dot_tn(uw[...], hidden[...]))
+    early.put(dot_tn(normed_two[...], cot_first[...]), 0)
+    early.put(dot_tn(uw[...], hidden[...]), 72)
     early.start()
     scatter(0, ow)
     backward(0)
@@ -570,43 +567,38 @@
     backward(3)
     early.step(1)
     norm = normed[...]
-    late.put(0, jnp.concatenate([dot_tn(norm, cot_q[...]), dot_tn(norm, cot_k[...])], axis=1))
+    late.put(jnp.concatenate([dot_tn(norm, cot_q[...]), dot_tn(norm, cot_k[...])], axis=1), 0)
     c_proj = dot_tn(blended[...], cot_mid[...])
-    late.put(1, jnp.concatenate([dot_tn(norm, cot_v[...]), c_proj], axis=1))
+    late.put(jnp.concatenate([dot_tn(norm, cot_v[...]), c_proj], axis=1), 36)
     late.start()
     collapse_bias(0, WH, scores, strips)
     strip_sum.put(join_strips(strips, columns, index_rows))
     strip_sum.start()
-    late.step(0)
     early.step(2)
-    strip_sum.step(0)
-    late.step(1)
-    early.step(3)
     inputs_back(0)
     inputs_back(1)
+    late.step(0)
     scatter(1, gw)
-    late.step(2)
-    early.step(4)
-    late.step(3)
+    strip_sum.step(0)
+    early.step(3)
+    late.step(1)
+    fc1[...] = joined(tiles_of(e_out)[:72], 6)
+    fc2[...] = joined(tiles_of(e_out)[72:], 6)
     strip_sum.step(1)
     end(outward[0])
     for index in range(4):
         whole_quarter(out_field, index, out[0, index])
-    early.step(5)
-    fc1[...] = joined(tiles_of(e_out, 0), 6)
-    fc2[...] = joined(tiles_of(e_out, 1), 6)
-    late.step(4)
+    late.step(2)
     strip_sum.step(2)
+    finish_bias(strip_sum.get(), lanes, tall_table, bias)
     end(outward[1])
     for index in range(4):
         whole_quarter(grad_field, index, out[1, index])
-    late.step(5)
-    qkv[:, 0:384] = joined(tiles_of(l_out, 0), 3)
-    right = joined(tiles_of(l_out, 1), 3)
+    late.step(3)
+    qkv[:, 0:384] = joined(tiles_of(l_out)[:36], 3)
+    right = joined(tiles_of(l_out)[36:], 3)
     qkv[:, 384:576] = right[:, 0:C]
     proj[...] = right[:, C:]
-    strip_sum.step(3)
-    finish_bias(b_out, lanes, tall_table, bias)
 
 
 def whole_quarter(target, index, packed):
@@ -620,14 +612,13 @@
     return jnp.concatenate(cols, axis=1).astype(F32)
 
 
-def tiles_of(ref, half):
+def tiles_of(ref):
     n1 = ref.shape[3]
-    return [ref[half, i // (4 * n1), i // n1 % 4, i % n1] for i in range(12 * n1)]
-
-
-def finish_bias(b_in, lanes, tall_table, bias):
-    tiles = [b_in[t // B_TILES, t % B_TILES // 4, t % B_TILES % 4] for t in range(2 * B_TILES)]
-    runs = dot_nt(joined(tiles, 3).astype(BF16), lanes[...])
+    return [ref[i // (8 * n1), i // (2 * n1) % RING, i // n1 % 2, i % n1] for i in range(24 * n1)]
+
+
+def finish_bias(strip, lanes, tall_table, bias):
+    runs = dot_nt(strip.astype(BF16), lanes[...])
     for site in range(SITE):
         lev, a = site // WLAT, site % WLAT
         for other in range(WLEV):
@@ -677,9 +668,9 @@
             *[pltpu.VMEM(a.shape, a.dtype) for a in inputs],
             dma((len(inputs),)),
             pltpu.VMEM((2, 4, PACKED, 128), BF16),
-            pltpu.VMEM((2, 3, RING, E_TILES // 12, *TILE), BF16),
-            pltpu.VMEM((2, 3, RING, L_TILES // 12, *TILE), BF16),
-            pltpu.VMEM((2, 8, B_ROOM // 8, *TILE), BF16),
+            room(3, RING, 2, E_TILES // 24),
+            room(3, RING, 2, L_TILES // 24),
+            room(RING, 2, B_TILES // 8),
             pltpu.VMEM((2, 3, PACKED, 128), BF16),
             pltpu.VMEM((2, 4, PACKED, 128), BF16),
             pltpu.VMEM((2, 4, PACKED, 128), BF16),

time: 55.9 us -> 56.4 us (level)
  no operation moved by 1% of the time
where the time goes in v2:
time: 56.4 us; the launch traced here: 56.2 us
  Pallas kernels  55.4 us (98%)
  between operations  0.8 us (1%)
    pallas_call x1, Pallas kernels, per_device(): pl.pallas_call(functools.partial(block_kernel, n_lon, n_lat), out_shape=o...  53.8 us
    pallas_call x1, Pallas kernels, per_device(): pl.pallas_call(finish_kernel, out_shape=outputs, in_specs=[vmem] * len(ou...  1.6 us

profile of v2, /device:TPU:1, one launch (start us, length us, event | category | flops | bytes accessed | tf_op | source)
XLA Modules:
  0.0 56.2 jit_solution(16203490458232896555)
XLA Ops:
  0.6 53.8 %block.1 = (bf16[12,6,8,192]{3,2,1,0:T(8,128)(2,1)S(1)}, bf16[12,6,8,192]{3,2,1,0:T(8,128)(2,1)S(1)}, f32[192,576]{1,0:T(8,128)S(1)}, f32[192,192]{1,0:T(8,128)S...) custom-call(bf16[12,6,8,192]{3,2,1,0:T(8,128)(2,1)} %refs_0_.1, ...), custom_call_target="tpu_custom_call" | custom-call | tf_op jit(solution)/shard_map/block/pallas_call | solution.py:662
  54.5 1.6 %finish.1 = (bf16[12,6,8,192]{3,2,1,0:T(8,128)(2,1)}, bf16[12,6,8,192]{3,2,1,0:T(8,128)(2,1)}, f32[192,576]{1,0:T(8,128)}, f32[192,192]{1,0:T(8,128)}, f32[192,7...) custom-call(bf16[12,6,8,192]{3,2,1,0:T(8,128)(2,1)S(1)} %get-tuple-element.21.refs_0_, ...), custom_call_target="tpu_custom_call" | custom-call | tf_op jit(solution)/shard_map/finish/pallas_call | solution.py:704

commit v3 on v2

--- a/solution.py
+++ b/solution.py
@@ -156,6 +156,7 @@
     def __init__(self, n_lon, n_lat):
         self.lon, self.lat = lax.axis_index("lon"), lax.axis_index("lat")
         self.chip, self.core = place_of(self.lon, self.lat)
+        self.sibling = (self.lon + 1 - 2 * self.core, self.lat)
         self.slot = [[lax.rem(c + k, RING) for k in range(RING)] for c in self.chip]
         chips = [[moved(self.chip, axis, k) for k in range(RING)] for axis in range(3)]
         self.along = [[device_at(chip, self.core) for chip in ring] for ring in chips]
@@ -279,6 +280,90 @@
             begin(self.phase(at + 1))
 
 
+class PairSum:
+    def __init__(self, here, out, refs):
+        self.here, self.out = here, out
+        self.src, self.other, self.a1, self.r1, self.x2, self.x3, self.send, self.recv = refs
+
+    @staticmethod
+    def scratch(tiles):
+        n1 = tiles // 24
+        dma = pltpu.SemaphoreType.DMA
+        return [
+            room(2, tiles // 2), room(tiles // 2),
+            room(3, RING, n1), room(3, RING - 1, n1), room(3, RING, n1), room(3, RING, n1),
+            dma((6,)), dma((6,)),
+        ]
+
+    def put(self, block, first):
+        each = self.src.shape[1]
+        for at, tile in enumerate(tiles_in(block), first):
+            self.src[at // each, at % each] = tile
+
+    def get(self):
+        n1 = self.a1.shape[2]
+        return [self.out[i // (12 * n1), i // (4 * n1) % 3, i // n1 % 4, i % n1] for i in range(24 * n1)]
+
+    def copies(self, at, axis_of, source, target):
+        made = []
+        for t in range(3):
+            axis = (t + axis_of) % 3
+            slot = self.here.slot[axis]
+            for k in range(1, RING):
+                made.append(
+                    remote(
+                        source(t, slot[k], slot[0]), target(t, k - 1, slot[0]),
+                        self.send.at[at], self.recv.at[at], self.here.along[axis][k],
+                    )
+                )
+        return made
+
+    def phase(self, at):
+        core = self.here.core
+        if at == 0:
+            return [remote(self.src.at[1 - core], self.other, self.send.at[0], self.recv.at[0], self.here.sibling)]
+        if at == 1:
+            return self.copies(1, 0, lambda t, to, me: self.a1.at[t, to], lambda t, k, me: self.r1.at[t, k])
+        if at == 2:
+            return self.copies(2, 1, lambda t, to, me: self.x2.at[t, me], lambda t, k, me: self.x2.at[t, me])
+        if at == 3:
+            return self.copies(3, 2, lambda t, to, me: self.x3.at[t, me], lambda t, k, me: self.x3.at[t, me])
+        if at == 4:
+            out = self.out.at[core]
+            return self.copies(4, 0, lambda t, to, me: out.at[t, me], lambda t, k, me: out.at[t, me])
+        return [remote(self.out.at[core], self.out.at[core], self.send.at[5], self.recv.at[5], self.here.sibling)]
+
+    def start(self):
+        begin(self.phase(0))
+
+    def step(self, at):
+        like = self.other if at in (0, 5) else self.r1
+        wait_bytes(like, self.recv.at[at])
+        wait_bytes(like, self.send.at[at])
+        core = self.here.core
+        if at == 0:
+            total = self.src[core].astype(F32) + self.other[...].astype(F32)
+            self.a1[...] = total.astype(BF16).reshape(self.a1.shape)
+        for t in range(3):
+            one, two, three = (self.here.slot[(t + i) % 3][0] for i in range(3))
+            if at == 1:
+                total = self.a1[t, one].astype(F32)
+                for k in range(RING - 1):
+                    total = total + self.r1[t, k].astype(F32)
+                self.x2[t, two] = total.astype(BF16)
+            if at in (2, 3):
+                came = self.x2 if at == 2 else self.x3
+                total = came[t, 0].astype(F32)
+                for k in range(1, RING):
+                    total = total + came[t, k].astype(F32)
+                if at == 2:
+                    self.x3[t, three] = total.astype(BF16)
+                else:
+                    self.out[core, t, one] = total.astype(BF16)
+        if at < 5:
+            begin(self.phase(at + 1))
+
+
 class BiasSum:
     def __init__(self, here, out, refs):
         self.here, self.out = here, out
@@ -435,9 +520,9 @@
         places_in, places_out, lanes,
     ) = refs[26:61]
     here = Here(n_lon, n_lat)
-    early = WeightSum(here, e_out, refs[61:67])
-    late = WeightSum(here, l_out, refs[67:73])
-    strip_sum = BiasSum(here, b_out, refs[73:78])
+    early = PairSum(here, e_out, refs[61:69])
+    late = WeightSum(here, l_out, refs[69:75])
+    strip_sum = BiasSum(here, b_out, refs[75:80])
 
     loads = [
         pltpu.make_async_copy(src, dst, load_sem.at[i]) for i, (src, dst) in enumerate(zip(loaded, refs[16:25]))
@@ -579,16 +664,18 @@
     inputs_back(1)
     late.step(0)
     scatter(1, gw)
+    early.step(3)
     strip_sum.step(0)
-    early.step(3)
     late.step(1)
-    fc1[...] = joined(tiles_of(e_out)[:72], 6)
-    fc2[...] = joined(tiles_of(e_out)[72:], 6)
+    early.step(4)
     strip_sum.step(1)
     end(outward[0])
     for index in range(4):
         whole_quarter(out_field, index, out[0, index])
     late.step(2)
+    early.step(5)
+    fc1[...] = joined(early.get()[:72], 6)
+    fc2[...] = joined(early.get()[72:], 6)
     strip_sum.step(2)
     finish_bias(strip_sum.get(), lanes, tall_table, bias)
     end(outward[1])
@@ -668,7 +755,7 @@
             *[pltpu.VMEM(a.shape, a.dtype) for a in inputs],
             dma((len(inputs),)),
             pltpu.VMEM((2, 4, PACKED, 128), BF16),
-            room(3, RING, 2, E_TILES // 24),
+            room(2, 3, RING, E_TILES // 24),
             room(3, RING, 2, L_TILES // 24),
             room(RING, 2, B_TILES // 8),
             pltpu.VMEM((2, 3, PACKED, 128), BF16),
@@ -692,7 +779,7 @@
             pltpu.VMEM((TOK, TOK), BF16),
             pltpu.VMEM((TOK, TOK), BF16),
             pltpu.VMEM((STRIP, LANES), BF16),
-            *WeightSum.scratch(E_TILES),
+            *PairSum.scratch(E_TILES),
             *WeightSum.scratch(L_TILES),
             *BiasSum.scratch(),
         ],

time: 56.4 us -> 54.3 us (0.963)
  Pallas kernels: 55.4 us -> 53.3 us
    pallas_call x1, Pallas kernels: 53.8 us -> 51.7 us  [per_device(): pl.pallas_call(functools.partial(block_kernel, n_lon, n_lat), out_shape=o...]
where the time goes in v3:
time: 54.3 us; the launch traced here: 54.1 us
  Pallas kernels  53.3 us (98%)
  between operations  0.8 us (1%)
    pallas_call x1, Pallas kernels, per_device(): pl.pallas_call(functools.partial(block_kernel, n_lon, n_lat), out_shape=o...  51.7 us
    pallas_call x1, Pallas kernels, per_device(): pl.pallas_call(finish_kernel, out_shape=outputs, in_specs=[vmem] * len(ou...  1.6 us

profile of v3, /device:TPU:1, one launch (start us, length us, event | category | flops | bytes accessed | tf_op | source)
XLA Modules:
  0.0 54.1 jit_solution(11684940011449779116)
XLA Ops:
  0.6 51.7 %block.1 = (bf16[12,6,8,192]{3,2,1,0:T(8,128)(2,1)S(1)}, bf16[12,6,8,192]{3,2,1,0:T(8,128)(2,1)S(1)}, f32[192,576]{1,0:T(8,128)S(1)}, f32[192,192]{1,0:T(8,128)S...) custom-call(bf16[12,6,8,192]{3,2,1,0:T(8,128)(2,1)} %refs_0_.1, ...), custom_call_target="tpu_custom_call" | custom-call | tf_op jit(solution)/shard_map/block/pallas_call | solution.py:749
  52.4 1.6 %finish.1 = (bf16[12,6,8,192]{3,2,1,0:T(8,128)(2,1)}, bf16[12,6,8,192]{3,2,1,0:T(8,128)(2,1)}, f32[192,576]{1,0:T(8,128)}, f32[192,192]{1,0:T(8,128)}, f32[192,7...) custom-call(bf16[12,6,8,192]{3,2,1,0:T(8,128)(2,1)S(1)} %get-tuple-element.21.refs_0_, ...), custom_call_target="tpu_custom_call" | custom-call | tf_op jit(solution)/shard_map/finish/pallas_call | solution.py:791

commit v4 on v3

--- a/solution.py
+++ b/solution.py
@@ -38,7 +38,9 @@
 B_TILES = 40
 B_LEFT = STRIP - 256
 B_ROWS = 48
-PACKED = 224
+CHUNK = QUAD // 2
+PAIR = 4 * CHUNK
+PACKED = 112
 TILE = (16, 128)
 BF16 = jnp.bfloat16
 F32 = jnp.float32
@@ -48,11 +50,11 @@
 
 def token_places():
     w, o, lev, a = np.meshgrid(
-        np.arange(LWIN), np.arange(WLON), np.arange(WLEV), np.arange(WLAT), indexing="ij"
+        np.arange(2), np.arange(WLON), np.arange(WLEV), np.arange(WLAT), indexing="ij"
     )
-    quarter = (o // 6) * 2 + a // 3
-    level = (2 * w + lev + 1) % LEV
-    return (quarter * QUAD + ((o % 6) * 3 + a % 3) * LEV + level).reshape(TOK).astype(np.int32)
+    site = (o % 6) * 3 + a % 3
+    row = (site % 9) * 8 + (site // 9) * 4 + 2 * w + lev
+    return (((o // 6) * 2 + a // 3) * CHUNK + row).reshape(PAIR).astype(np.int32)
 
 
 def lane_places():
@@ -112,24 +114,35 @@
     return found
 
 
-def quarter(ref, index):
+def split(ref, index):
     part = ref[pl.ds((index // 2) * 6, 6), pl.ds((index % 2) * 3, 3)]
-    return part.astype(F32).reshape(QUAD, C)
+    part = pltpu.roll(part.astype(F32).reshape(18, LEV, C), LEV - 1, 1)
+    low, high = part[:9], part[9:]
+    upper = lax.broadcasted_iota(jnp.int32, low.shape, 1) < LEV // 2
+    first = jnp.where(upper, low, pltpu.roll(high, LEV // 2, 1))
+    second = jnp.where(upper, pltpu.roll(low, LEV // 2, 1), high)
+    return first.reshape(CHUNK, C), second.reshape(CHUNK, C)
+
+
+def merge(ref, index, chunks):
+    first, second = (chunk.reshape(9, LEV, C) for chunk in chunks)
+    upper = lax.broadcasted_iota(jnp.int32, first.shape, 1) < LEV // 2
+    low = jnp.where(upper, first, pltpu.roll(second, LEV // 2, 1))
+    high = jnp.where(upper, pltpu.roll(first, LEV // 2, 1), second)
+    part = pltpu.roll(jnp.concatenate([low, high], axis=0), 1, 1)
+    ref[pl.ds((index // 2) * 6, 6), pl.ds((index % 2) * 3, 3)] = part.reshape(6, 3, LEV, C).astype(BF16)
 
 
 def pack(value):
-    half = QUAD // 2
-    rest = jnp.concatenate([value[:half, 128:], value[half:, 128:]], axis=1)
-    blank = jnp.zeros((PACKED - QUAD - half, 128), F32)
-    return jnp.concatenate([value[:, :128], rest, blank], axis=0).astype(BF16)
+    rest = jnp.concatenate([value[:40, 128:], value[32:, 128:]], axis=1)
+    return jnp.concatenate([value[:, :128], rest], axis=0).astype(BF16)
 
 
 def unpack(value):
-    half = QUAD // 2
     wide = value.astype(F32)
-    rest = wide[QUAD : QUAD + half]
-    right = jnp.concatenate([rest[:, :64], rest[:, 64:]], axis=0)
-    return jnp.concatenate([wide[:QUAD], right], axis=1)
+    rest = wide[CHUNK:]
+    right = jnp.concatenate([rest[:, :64], rest[8:, 64:]], axis=0)
+    return jnp.concatenate([wide[:CHUNK], right], axis=1)
 
 
 def place_of(lon, lat):
@@ -177,9 +190,9 @@
             self.across[step] = ((to_lon, to_lat), (to_lon, self.lat), (self.lon, to_lat))
 
     def greet(self):
-        others = [*self.across[-1], *self.across[1], self.facing]
+        others = [*self.across[-1], *self.across[1], self.sibling]
         for axis in range(3):
-            others += [device for device, _, _ in self.eight[axis]]
+            others += [device for device, _, _ in self.eight[axis][1:]]
         barrier = pltpu.get_barrier_semaphore()
         for device in others:
             pl.semaphore_signal(barrier, inc=1, device_id=device, device_id_type=MESH)
@@ -514,55 +527,66 @@
     out_field, grad_field, qkv, proj, fc1, fc2, bias = refs[9:16]
     field, cot, w_qkv, w_proj, w_fc1, w_fc2, table, columns, index_rows, load_sem = refs[16:26]
     (
-        out, e_out, l_out, b_out, sent, came, back, halo_send, halo_recv,
+        out, e_out, l_out, b_out, sent, came, cot_sent, cot_came, back, halo_send, halo_recv,
         xw, uw, scores, normed, query, key, value, unit, rate, blended, normed_two, hidden,
         cot_first, cot_mid, cot_q, cot_k, cot_v, ow, gw, tall_table, gathered, strips, w3,
         places_in, places_out, lanes,
-    ) = refs[26:61]
+    ) = refs[26:63]
     here = Here(n_lon, n_lat)
-    early = PairSum(here, e_out, refs[61:69])
-    late = WeightSum(here, l_out, refs[69:75])
-    strip_sum = BiasSum(here, b_out, refs[75:80])
+    early = PairSum(here, e_out, refs[63:71])
+    late = WeightSum(here, l_out, refs[71:77])
+    strip_sum = BiasSum(here, b_out, refs[77:82])
 
     loads = [
         pltpu.make_async_copy(src, dst, load_sem.at[i]) for i, (src, dst) in enumerate(zip(loaded, refs[16:25]))
     ]
-    begin(loads)
+    loads[0].start()
     greeted = here.greet()
+    begin(loads[6:9])
     loads[0].wait()
     for index in range(3):
-        sent[0, index] = pack(quarter(field, index))
+        for part, chunk in enumerate(split(field, index)):
+            sent[part, index] = pack(chunk)
     greeted()
     inward = [
         halo(here, sent.at[i], came.at[i], halo_send.at[i], halo_recv.at[i], -1) for i in range(2)
     ]
+    cot_inward = halo(here, cot_sent, cot_came, halo_send.at[2], halo_recv.at[2], -1)
     outward = [
-        halo(here, back.at[i], out.at[i], halo_send.at[2 + i], halo_recv.at[2 + i], 1) for i in range(2)
+        halo(here, back.at[i], out.at[i], halo_send.at[3 + i], halo_recv.at[3 + i], 1) for i in range(2)
     ]
     begin(inward[0])
+    begin(inward[1])
+    begin(loads[1:6])
     end(loads[6:9])
     lanes[...] = one_hot(columns[0:STRIP, 3:4], STRIP, LANES)
     last_lat = here.lat == n_lat - 1
     expand_bias(last_lat, table, columns, index_rows, lanes, tall_table, gathered, strips, scores)
-    places_in[...] = one_hot(columns[:, 0:1], TOK, TOK)
-    places_out[...] = one_hot(index_rows[0:1, :], TOK, TOK)
+    places_in[...] = one_hot(columns[0:PAIR, 0:1], PAIR, PAIR)
+    places_out[...] = one_hot(index_rows[0:1, 0:PAIR], PAIR, PAIR)
     loads[1].wait()
     for index in range(3):
-        sent[1, index] = pack(quarter(cot, index))
+        for part, chunk in enumerate(split(cot, index)):
+            cot_sent[index, part] = pack(chunk)
+    own = [split(ref, 3) for ref in (field, cot)]
     loads[2].wait()
     for third in range(3):
         w3[third] = w_qkv[:, third * C : (third + 1) * C]
 
-    def gather(kind, ref):
-        parts = [quarter(ref, 3)] + [unpack(came[kind, i]) for i in range(1, 4)]
-        whole = jnp.concatenate(parts, axis=0).astype(BF16)
-        return dot(places_in[...], whole).astype(BF16)
+    def gather(kind, part):
+        if kind:
+            arrived = [cot_came[i, part] for i in range(1, 4)]
+        else:
+            arrived = [came[part, i] for i in range(1, 4)]
+        parts = [own[kind][part]] + [unpack(value) for value in arrived]
+        return dot(places_in[...], jnp.concatenate(parts, axis=0).astype(BF16)).astype(BF16)
 
     def scatter(kind, ref):
-        whole = dot(places_out[...], ref[...])
-        out[kind, 3] = pack(whole[:QUAD])
-        for i in range(1, 4):
-            back[kind, i] = pack(whole[i * QUAD : (i + 1) * QUAD])
+        for part in range(2):
+            whole = dot(places_out[...], ref[part * PAIR : (part + 1) * PAIR, :])
+            out[kind, 3, part] = pack(whole[:CHUNK])
+            for i in range(1, 4):
+                back[kind, i, part] = pack(whole[i * CHUNK : (i + 1) * CHUNK])
         begin(outward[kind])
 
     def places(w):
@@ -631,14 +655,17 @@
         c_x = layer_norm_back(c_norm, unit[rows, :], rate[rows, :]).astype(BF16)
         gw[rows, :] = (cot_mid[rows, :].astype(F32) + c_x.astype(F32)).astype(BF16)
 
-    end(inward[0])
-    begin(inward[1])
-    xw[...] = gather(0, field)
-    for w in range(LWIN):
-        attend(w)
+    for part in range(2):
+        end(inward[part])
+        xw[part * PAIR : (part + 1) * PAIR, :] = gather(0, part)
+        if part:
+            begin(cot_inward)
+        attend(2 * part)
+        attend(2 * part + 1)
     end(loads[3:6])
-    end(inward[1])
-    uw[...] = gather(1, cot)
+    end(cot_inward)
+    for part in range(2):
+        uw[part * PAIR : (part + 1) * PAIR, :] = gather(1, part)
     feed(0)
     feed(1)
     early.put(dot_tn(normed_two[...], cot_first[...]), 0)
@@ -671,7 +698,7 @@
     strip_sum.step(1)
     end(outward[0])
     for index in range(4):
-        whole_quarter(out_field, index, out[0, index])
+        merge(out_field, index, [unpack(out[0, index, part]) for part in range(2)])
     late.step(2)
     early.step(5)
     fc1[...] = joined(early.get()[:72], 6)
@@ -680,17 +707,12 @@
     finish_bias(strip_sum.get(), lanes, tall_table, bias)
     end(outward[1])
     for index in range(4):
-        whole_quarter(grad_field, index, out[1, index])
+        merge(grad_field, index, [unpack(out[1, index, part]) for part in range(2)])
     late.step(3)
     qkv[:, 0:384] = joined(tiles_of(l_out)[:36], 3)
     right = joined(tiles_of(l_out)[36:], 3)
     qkv[:, 384:576] = right[:, 0:C]
     proj[...] = right[:, C:]
-
-
-def whole_quarter(target, index, packed):
-    part = unpack(packed).reshape(6, 3, LEV, C).astype(BF16)
-    target[pl.ds((index // 2) * 6, 6), pl.ds((index % 2) * 3, 3)] = part
 
 
 def joined(tiles, columns):
@@ -754,15 +776,17 @@
         scratch_shapes=[
             *[pltpu.VMEM(a.shape, a.dtype) for a in inputs],
             dma((len(inputs),)),
-            pltpu.VMEM((2, 4, PACKED, 128), BF16),
+            pltpu.VMEM((2, 4, 2, PACKED, 128), BF16),
             room(2, 3, RING, E_TILES // 24),
             room(3, RING, 2, L_TILES // 24),
             room(RING, 2, B_TILES // 8),
             pltpu.VMEM((2, 3, PACKED, 128), BF16),
             pltpu.VMEM((2, 4, PACKED, 128), BF16),
-            pltpu.VMEM((2, 4, PACKED, 128), BF16),
-            dma((4, 3)),
-            dma((4, 3)),
+            pltpu.VMEM((3, 2, PACKED, 128), BF16),
+            pltpu.VMEM((4, 2, PACKED, 128), BF16),
+            pltpu.VMEM((2, 4, 2, PACKED, 128), BF16),
+            dma((5, 3)),
+            dma((5, 3)),
             *wide(BF16, 2),
             pltpu.VMEM((LWIN * STACK, WIN), F32),
             *wide(BF16, 4),
@@ -776,8 +800,8 @@
             pltpu.VMEM((SITE * WH, STRIP), F32),
             pltpu.VMEM((WH * 2 * SITE, LANES), F32),
             pltpu.VMEM((3, C, C), BF16),
-            pltpu.VMEM((TOK, TOK), BF16),
-            pltpu.VMEM((TOK, TOK), BF16),
+            pltpu.VMEM((PAIR, PAIR), BF16),
+            pltpu.VMEM((PAIR, PAIR), BF16),
             pltpu.VMEM((STRIP, LANES), BF16),
             *PairSum.scratch(E_TILES),
             *WeightSum.scratch(L_TILES),

time: 54.3 us -> 56.3 us (1.037)
  Pallas kernels: 53.3 us -> 55.4 us
    pallas_call x1, Pallas kernels: 51.7 us -> 53.8 us  [per_device(): pl.pallas_call(functools.partial(block_kernel, n_lon, n_lat), out_shape=o...]
where the time goes in v4:
time: 56.3 us; the launch traced here: 56.2 us
  Pallas kernels  55.4 us (98%)
  between operations  0.82 us (1%)
    pallas_call x1, Pallas kernels, per_device(): pl.pallas_call(functools.partial(block_kernel, n_lon, n_lat), out_shape=o...  53.8 us
    pallas_call x1, Pallas kernels, per_device(): pl.pallas_call(finish_kernel, out_shape=outputs, in_specs=[vmem] * len(ou...  1.6 us

profile of v4, /device:TPU:1, one launch (start us, length us, event | category | flops | bytes accessed | tf_op | source)
XLA Modules:
  0.0 56.2 jit_solution(17657703440974939104)
XLA Ops:
  0.6 53.8 %block.1 = (bf16[12,6,8,192]{3,2,1,0:T(8,128)(2,1)S(1)}, bf16[12,6,8,192]{3,2,1,0:T(8,128)(2,1)S(1)}, f32[192,576]{1,0:T(8,128)S(1)}, f32[192,192]{1,0:T(8,128)S...) custom-call(bf16[12,6,8,192]{3,2,1,0:T(8,128)(2,1)} %refs_0_.1, ...), custom_call_target="tpu_custom_call" | custom-call | tf_op jit(solution)/shard_map/block/pallas_call | solution.py:771
  54.4 1.6 %finish.1 = (bf16[12,6,8,192]{3,2,1,0:T(8,128)(2,1)}, bf16[12,6,8,192]{3,2,1,0:T(8,128)(2,1)}, f32[192,576]{1,0:T(8,128)}, f32[192,192]{1,0:T(8,128)}, f32[192,7...) custom-call(bf16[12,6,8,192]{3,2,1,0:T(8,128)(2,1)S(1)} %get-tuple-element.21.refs_0_, ...), custom_call_target="tpu_custom_call" | custom-call | tf_op jit(solution)/shard_map/finish/pallas_call | solution.py:815

commit v5 on v4

--- a/solution.py
+++ b/solution.py
@@ -530,12 +530,12 @@
         out, e_out, l_out, b_out, sent, came, cot_sent, cot_came, back, halo_send, halo_recv,
         xw, uw, scores, normed, query, key, value, unit, rate, blended, normed_two, hidden,
         cot_first, cot_mid, cot_q, cot_k, cot_v, ow, gw, tall_table, gathered, strips, w3,
-        places_in, places_out, lanes,
-    ) = refs[26:63]
+        places_in, places_out, lanes, slope, unit_two, rate_two,
+    ) = refs[26:66]
     here = Here(n_lon, n_lat)
-    early = PairSum(here, e_out, refs[63:71])
-    late = WeightSum(here, l_out, refs[71:77])
-    strip_sum = BiasSum(here, b_out, refs[77:82])
+    early = PairSum(here, e_out, refs[66:74])
+    late = WeightSum(here, l_out, refs[74:80])
+    strip_sum = BiasSum(here, b_out, refs[80:85])
 
     loads = [
         pltpu.make_async_copy(src, dst, load_sem.at[i]) for i, (src, dst) in enumerate(zip(loaded, refs[16:25]))
@@ -623,13 +623,18 @@
         hid = (first * phi).astype(BF16)
         hidden[rows, :] = hid
         bell = jnp.exp2(first * first * (-0.5 * LOG2E)) * (1.0 / math.sqrt(2.0 * math.pi))
-        slope = phi + first * bell
+        slope[rows, :] = phi + first * bell
+        unit_two[rows, :] = unit_m
+        rate_two[rows, :] = rate_m
         ow[rows, :] = (middle + dot_nt(hid, w_fc2[...])).astype(BF16)
+
+    def feed_back(w):
+        rows = pl.ds(w * 2 * WIN, 2 * WIN)
         up = uw[rows, :]
-        c_first = (dot(up, w_fc2[...]).astype(BF16).astype(F32) * slope).astype(BF16)
+        c_first = (dot(up, w_fc2[...]).astype(BF16).astype(F32) * slope[rows, :]).astype(BF16)
         cot_first[rows, :] = c_first
         c_norm = dot_nt(c_first, w_fc1[...]).astype(BF16).astype(F32)
-        c_mid = layer_norm_back(c_norm, unit_m, rate_m).astype(BF16).astype(F32)
+        c_mid = layer_norm_back(c_norm, unit_two[rows, :], rate_two[rows, :]).astype(BF16).astype(F32)
         cot_mid[rows, :] = (up.astype(F32) + c_mid).astype(BF16)
 
     def backward(w):
@@ -658,20 +663,21 @@
     for part in range(2):
         end(inward[part])
         xw[part * PAIR : (part + 1) * PAIR, :] = gather(0, part)
-        if part:
+        if not part:
             begin(cot_inward)
         attend(2 * part)
         attend(2 * part + 1)
     end(loads[3:6])
+    feed(0)
+    feed(1)
+    scatter(0, ow)
     end(cot_inward)
     for part in range(2):
         uw[part * PAIR : (part + 1) * PAIR, :] = gather(1, part)
-    feed(0)
-    feed(1)
+        feed_back(part)
     early.put(dot_tn(normed_two[...], cot_first[...]), 0)
     early.put(dot_tn(uw[...], hidden[...]), 72)
     early.start()
-    scatter(0, ow)
     backward(0)
     backward(1)
     early.step(0)
@@ -803,6 +809,9 @@
             pltpu.VMEM((PAIR, PAIR), BF16),
             pltpu.VMEM((PAIR, PAIR), BF16),
             pltpu.VMEM((STRIP, LANES), BF16),
+            pltpu.VMEM((TOK, HIDDEN), F32),
+            *wide(F32),
+            pltpu.VMEM((TOK, 1), F32),
             *PairSum.scratch(E_TILES),
             *WeightSum.scratch(L_TILES),
             *BiasSum.scratch(),

time: 56.3 us -> 52.1 us (0.925)
  Pallas kernels: 55.4 us -> 51.2 us
    pallas_call x1, Pallas kernels: 53.8 us -> 49.6 us  [per_device(): pl.pallas_call(functools.partial(block_kernel, n_lon, n_lat), out_shape=o...]
where the time goes in v5:
time: 52.1 us; the launch traced here: 52 us
  Pallas kernels  51.2 us (98%)
  between operations  0.82 us (2%)
    pallas_call x1, Pallas kernels, per_device(): pl.pallas_call(functools.partial(block_kernel, n_lon, n_lat), out_shape=o...  49.6 us
    pallas_call x1, Pallas kernels, per_device(): pl.pallas_call(finish_kernel, out_shape=outputs, in_specs=[vmem] * len(ou...  1.6 us

profile of v5, /device:TPU:1, one launch (start us, length us, event | category | flops | bytes accessed | tf_op | source)
XLA Modules:
  0.0 52.0 jit_solution(2901929750510002551)
XLA Ops:
  0.6 49.6 %block.1 = (bf16[12,6,8,192]{3,2,1,0:T(8,128)(2,1)S(1)}, bf16[12,6,8,192]{3,2,1,0:T(8,128)(2,1)S(1)}, f32[192,576]{1,0:T(8,128)S(1)}, f32[192,192]{1,0:T(8,128)S...) custom-call(bf16[12,6,8,192]{3,2,1,0:T(8,128)(2,1)} %refs_0_.1, ...), custom_call_target="tpu_custom_call" | custom-call | tf_op jit(solution)/shard_map/block/pallas_call | solution.py:777
  50.2 1.6 %finish.1 = (bf16[12,6,8,192]{3,2,1,0:T(8,128)(2,1)}, bf16[12,6,8,192]{3,2,1,0:T(8,128)(2,1)}, f32[192,576]{1,0:T(8,128)}, f32[192,192]{1,0:T(8,128)}, f32[192,7...) custom-call(bf16[12,6,8,192]{3,2,1,0:T(8,128)(2,1)S(1)} %get-tuple-element.21.refs_0_, ...), custom_call_target="tpu_custom_call" | custom-call | tf_op jit(solution)/shard_map/finish/pallas_call | solution.py:824

commit v6 on v5

--- a/solution.py
+++ b/solution.py
@@ -670,7 +670,6 @@
     end(loads[3:6])
     feed(0)
     feed(1)
-    scatter(0, ow)
     end(cot_inward)
     for part in range(2):
         uw[part * PAIR : (part + 1) * PAIR, :] = gather(1, part)
@@ -680,10 +679,9 @@
     early.start()
     backward(0)
     backward(1)
+    backward(2)
     early.step(0)
-    backward(2)
     backward(3)
-    early.step(1)
     norm = normed[...]
     late.put(jnp.concatenate([dot_tn(norm, cot_q[...]), dot_tn(norm, cot_k[...])], axis=1), 0)
     c_proj = dot_tn(blended[...], cot_mid[...])
@@ -692,28 +690,30 @@
     collapse_bias(0, WH, scores, strips)
     strip_sum.put(join_strips(strips, columns, index_rows))
     strip_sum.start()
-    early.step(2)
+    early.step(1)
     inputs_back(0)
     inputs_back(1)
     late.step(0)
     scatter(1, gw)
-    early.step(3)
+    scatter(0, ow)
+    early.step(2)
     strip_sum.step(0)
     late.step(1)
+    early.step(3)
+    strip_sum.step(1)
+    late.step(2)
     early.step(4)
-    strip_sum.step(1)
+    end(outward[1])
+    for index in range(4):
+        merge(grad_field, index, [unpack(out[1, index, part]) for part in range(2)])
     end(outward[0])
     for index in range(4):
         merge(out_field, index, [unpack(out[0, index, part]) for part in range(2)])
-    late.step(2)
+    strip_sum.step(2)
+    finish_bias(strip_sum.get(), lanes, tall_table, bias)
     early.step(5)
     fc1[...] = joined(early.get()[:72], 6)
     fc2[...] = joined(early.get()[72:], 6)
-    strip_sum.step(2)
-    finish_bias(strip_sum.get(), lanes, tall_table, bias)
-    end(outward[1])
-    for index in range(4):
-        merge(grad_field, index, [unpack(out[1, index, part]) for part in range(2)])
     late.step(3)
     qkv[:, 0:384] = joined(tiles_of(l_out)[:36], 3)
     right = joined(tiles_of(l_out)[36:], 3)

time: 52.1 us -> 51.7 us (level)
  no operation moved by 1% of the time
where the time goes in v6:
time: 51.7 us; the launch traced here: 51.6 us
  Pallas kernels  50.8 us (98%)
  between operations  0.82 us (2%)
    pallas_call x1, Pallas kernels, per_device(): pl.pallas_call(functools.partial(block_kernel, n_lon, n_lat), out_shape=o...  49.2 us
    pallas_call x1, Pallas kernels, per_device(): pl.pallas_call(finish_kernel, out_shape=outputs, in_specs=[vmem] * len(ou...  1.6 us

profile of v6, /device:TPU:1, one launch (start us, length us, event | category | flops | bytes accessed | tf_op | source)
XLA Modules:
  0.0 51.6 jit_solution(17268160034929125793)
XLA Ops:
  0.6 49.2 %block.1 = (bf16[12,6,8,192]{3,2,1,0:T(8,128)(2,1)S(1)}, bf16[12,6,8,192]{3,2,1,0:T(8,128)(2,1)S(1)}, f32[192,576]{1,0:T(8,128)S(1)}, f32[192,192]{1,0:T(8,128)S...) custom-call(bf16[12,6,8,192]{3,2,1,0:T(8,128)(2,1)} %refs_0_.1, ...), custom_call_target="tpu_custom_call" | custom-call | tf_op jit(solution)/shard_map/block/pallas_call | solution.py:777
  49.8 1.6 %finish.1 = (bf16[12,6,8,192]{3,2,1,0:T(8,128)(2,1)}, bf16[12,6,8,192]{3,2,1,0:T(8,128)(2,1)}, f32[192,576]{1,0:T(8,128)}, f32[192,192]{1,0:T(8,128)}, f32[192,7...) custom-call(bf16[12,6,8,192]{3,2,1,0:T(8,128)(2,1)S(1)} %get-tuple-element.21.refs_0_, ...), custom_call_target="tpu_custom_call" | custom-call | tf_op jit(solution)/shard_map/finish/pallas_call | solution.py:824

commit v7 on v6

--- a/solution.py
+++ b/solution.py
@@ -62,17 +62,12 @@
     return ((SHIFTS - 1 - d) * SITE + lev * WLAT + a).reshape(STRIP).astype(np.int32)
 
 
-def row_places():
-    wh, _, site = np.meshgrid(np.arange(WH), np.arange(2), np.arange(SITE), indexing="ij")
-    return (site * WH + wh).reshape(WH * 2 * SITE).astype(np.int32)
-
-
 def row_codes():
-    _, w, p, lev, a = np.meshgrid(
-        np.arange(HEADS), np.arange(LWIN), np.arange(2), np.arange(WLEV), np.arange(WLAT), indexing="ij"
+    lev, a, _, w = np.meshgrid(
+        np.arange(WLEV), np.arange(WLAT), np.arange(HEADS), np.arange(LWIN), indexing="ij"
     )
-    code = lev + 2 * (a >= WLAT // 2) + 4 * (w == LWIN - 1) + 8 * (p == 0)
-    return code.reshape(WH * 2 * SITE).astype(np.int32)
+    code = lev + 2 * (a >= WLAT // 2) + 4 * (w == LWIN - 1)
+    return code.reshape(SITE * WH).astype(np.int32)
 
 
 def lane_codes():
@@ -478,29 +473,27 @@
             gathered[site * WH : (site + 1) * WH, other * RUN : (other + 1) * RUN] = tall_table[
                 :, start : start + RUN
             ]
-    moved = sum(dot(part, lanes[...]) for part in pieces(gathered[...], 3))
-    rows = one_hot(columns[:, 1:2], WH * 2 * SITE, SITE * WH)
-    moved = sum(dot(rows, part) for part in pieces(moved, 3))
-    code = columns[:, 2:3]
-    moved = jnp.where((code & 8) != 0, pltpu.roll(moved, LANES - SITE, 1), moved) * LOG2E
+    strip = sum(dot(part, lanes[...]) for part in pieces(gathered[...], 3)) * LOG2E
+    code = columns[0 : SITE * WH, 2:3]
     seen = jnp.where((code & 4) != 0, 1, 0) + jnp.where(last_lat, 2, 0)
     apart = (code ^ index_rows[2:3, 0:LANES]) & seen
-    strips[...] = jnp.where(apart != 0, MASKED, moved)
+    strip = jnp.where(apart != 0, MASKED, strip)
+    for c in range(LANES // 128):
+        strips[c] = strip[:, c * 128 : (c + 1) * 128]
 
     def one(wh, carry):
-        strip = strips[pl.ds(pl.multiple_of(wh * 2 * SITE, 8), 2 * SITE), :]
+        odd = jnp.concatenate([strips[c, pl.ds(wh, SITE, WH), :] for c in range(LANES // 128)], axis=1)
+        both = jnp.concatenate([pltpu.roll(odd, LANES - SITE, 1), odd], axis=0)
         start = lax.rem(wh, LWIN) * STACK + lax.div(wh, LWIN) * WIN
         for pair in range(WLON // 2):
             offset = (WLON - 2 - 2 * pair) * SITE
-            scores[pl.ds(pl.multiple_of(start + pair * 24, 8), 24), :] = strip[
-                :, offset : offset + WIN
-            ]
+            scores[pl.ds(pl.multiple_of(start + pair * 24, 8), 24), :] = both[:, offset : offset + WIN]
         return carry
 
     lax.fori_loop(0, WH, one, 0)
 
 
-def collapse_bias(first, last, scores, strips):
+def collapse_bias(scores, strips):
     def one(wh, carry):
         start = lax.rem(wh, LWIN) * STACK + lax.div(wh, LWIN) * WIN
         total = jnp.zeros((2 * SITE, LANES), F32)
@@ -509,17 +502,12 @@
             part = scores[pl.ds(pl.multiple_of(start + pair * 24, 8), 24), :]
             part = jnp.concatenate([part, jnp.zeros((2 * SITE, LANES - WIN), F32)], axis=1)
             total = total + (pltpu.roll(part, offset, 1) if offset else part)
-        strips[pl.ds(pl.multiple_of(wh * 2 * SITE, 8), 2 * SITE), :] = total
+        total = pltpu.roll(total[:SITE], SITE, 1) + total[SITE:]
+        for c in range(LANES // 128):
+            strips[c, pl.ds(wh, SITE, WH), :] = total[:, c * 128 : (c + 1) * 128]
         return carry
 
-    lax.fori_loop(first, last, one, 0)
-
-
-def join_strips(strips, columns, index_rows):
-    total = strips[...]
-    total = jnp.where((columns[:, 2:3] & 8) != 0, pltpu.roll(total, SITE, 1), total)
-    rows = one_hot(index_rows[1:2, :], SITE * WH, WH * 2 * SITE)
-    return sum(dot(rows, part) for part in pieces(total, 2))
+    lax.fori_loop(0, WH, one, 0)
 
 
 def block_kernel(n_lon, n_lat, *refs):
@@ -687,8 +675,8 @@
     c_proj = dot_tn(blended[...], cot_mid[...])
     late.put(jnp.concatenate([dot_tn(norm, cot_v[...]), c_proj], axis=1), 36)
     late.start()
-    collapse_bias(0, WH, scores, strips)
-    strip_sum.put(join_strips(strips, columns, index_rows))
+    collapse_bias(scores, strips)
+    strip_sum.put(jnp.concatenate([strips[c] for c in range(LANES // 128)], axis=1))
     strip_sum.start()
     early.step(1)
     inputs_back(0)
@@ -756,9 +744,8 @@
     vmem, hbm = pl.BlockSpec(memory_space=pltpu.VMEM), pl.BlockSpec(memory_space=pltpu.HBM)
     shape = jax.ShapeDtypeStruct
     dma = pltpu.SemaphoreType.DMA
-    rows = row_places()
-    columns = columns_of(token_places(), rows, row_codes(), lane_places())
-    index_rows = columns_of(token_places(), rows, lane_codes()).T.copy()
+    columns = columns_of(token_places(), [], row_codes(), lane_places())
+    index_rows = columns_of(token_places(), [], lane_codes()).T.copy()
     inputs = (
         field, cotangent, w_qkv, w_proj, w_fc1, w_fc2.T, bias_table[0].transpose(1, 0, 2), columns, index_rows
     )
@@ -804,7 +791,7 @@
             *wide(BF16, 6),
             pltpu.VMEM((WH, POS), F32),
             pltpu.VMEM((SITE * WH, STRIP), F32),
-            pltpu.VMEM((WH * 2 * SITE, LANES), F32),
+            pltpu.VMEM((LANES // 128, SITE * WH, 128), F32),
             pltpu.VMEM((3, C, C), BF16),
             pltpu.VMEM((PAIR, PAIR), BF16),
             pltpu.VMEM((PAIR, PAIR), BF16),

time: 51.7 us -> 52.5 us (1.015)
  Pallas kernels: 50.8 us -> 51.5 us
    pallas_call x1, Pallas kernels: 49.2 us -> 49.9 us  [per_device(): pl.pallas_call(functools.partial(block_kernel, n_lon, n_lat), out_shape=o...]
where the time goes in v7:
time: 52.5 us; the launch traced here: 52.3 us
  Pallas kernels  51.5 us (98%)
  between operations  0.8 us (2%)
    pallas_call x1, Pallas kernels, per_device(): pl.pallas_call(functools.partial(block_kernel, n_lon, n_lat), out_shape=o...  49.9 us
    pallas_call x1, Pallas kernels, per_device(): pl.pallas_call(finish_kernel, out_shape=outputs, in_specs=[vmem] * len(ou...  1.6 us

profile of v7, /device:TPU:1, one launch (start us, length us, event | category | flops | bytes accessed | tf_op | source)
XLA Modules:
  0.0 52.3 jit_solution(17827169771579723049)
XLA Ops:
  0.6 49.9 %block.1 = (bf16[12,6,8,192]{3,2,1,0:T(8,128)(2,1)S(1)}, bf16[12,6,8,192]{3,2,1,0:T(8,128)(2,1)S(1)}, f32[192,576]{1,0:T(8,128)S(1)}, f32[192,192]{1,0:T(8,128)S...) custom-call(bf16[12,6,8,192]{3,2,1,0:T(8,128)(2,1)} %refs_0_.1, ...), custom_call_target="tpu_custom_call" | custom-call | tf_op jit(solution)/shard_map/block/pallas_call | solution.py:764
  50.6 1.6 %finish.1 = (bf16[12,6,8,192]{3,2,1,0:T(8,128)(2,1)}, bf16[12,6,8,192]{3,2,1,0:T(8,128)(2,1)}, f32[192,576]{1,0:T(8,128)}, f32[192,192]{1,0:T(8,128)}, f32[192,7...) custom-call(bf16[12,6,8,192]{3,2,1,0:T(8,128)(2,1)S(1)} %get-tuple-element.21.refs_0_, ...), custom_call_target="tpu_custom_call" | custom-call | tf_op jit(solution)/shard_map/finish/pallas_call | solution.py:811

commit v8 on v6

--- a/solution.py
+++ b/solution.py
@@ -33,6 +33,7 @@
 LOG2E = math.log2(math.e)
 SCALE = 1.0 / math.sqrt(C // HEADS)
 RING = 4
+FAR_FIRST = (2, 1, 3)
 E_TILES = 144
 L_TILES = 72
 B_TILES = 40
@@ -177,7 +178,7 @@
         self.eight = []
         for axis in range(3):
             found = []
-            for k in range(RING):
+            for k in FAR_FIRST + (0,):
                 if k:
                     found.append((self.along[axis][k], self.slot[axis][k], self.core))
                 found.append((device_at(chips[axis][k], other), self.slot[axis][k], other))
@@ -192,7 +193,7 @@
     def greet(self):
         others = [*self.across[-1], *self.across[1], self.sibling]
         for axis in range(3):
-            others += [device for device, _, _ in self.eight[axis][1:]]
+            others += [device for device, _, _ in self.eight[axis][:-1]]
         barrier = pltpu.get_barrier_semaphore()
         for device in others:
             pl.semaphore_signal(barrier, inc=1, device_id=device, device_id_type=MESH)
@@ -201,7 +202,7 @@
 
 def halo(here, source, target, send, recv, step):
     copies = []
-    for index in range(3):
+    for index in (0, 2, 1):
         src = index if step < 0 else 3 - index
         device = here.across[step][index]
         copies.append(remote(source.at[src], target.at[3 - src], send.at[index], recv.at[index], device))
@@ -259,18 +260,21 @@
     def phase(self, at):
         here, made = self.here, []
         sems = self.send.at[at], self.recv.at[at]
-        for t in range(3):
-            if at in (0, 3):
-                mine = self.out.at[t, here.slot[t][0], here.core]
-                for k, (device, slot, core) in enumerate(here.eight[t]):
+        if at in (0, 3):
+            for k in range(7):
+                for t in range(3):
+                    device, slot, core = here.eight[t][k]
+                    mine = self.out.at[t, here.slot[t][0], here.core]
                     if at == 0:
                         made.append(remote(self.src.at[t, slot, core], self.r1.at[k, t], *sems, device))
                     else:
                         made.append(remote(mine, mine, *sems, device))
-            else:
-                axis = (t + at) % 3
-                mine = (self.x2 if at == 1 else self.x3).at[t, here.slot[axis][0]]
-                made += [remote(mine, mine, *sems, here.along[axis][k]) for k in range(1, RING)]
+        else:
+            for k in FAR_FIRST:
+                for t in range(3):
+                    axis = (t + at) % 3
+                    mine = (self.x2 if at == 1 else self.x3).at[t, here.slot[axis][0]]
+                    made.append(remote(mine, mine, *sems, here.along[axis][k]))
         return made
 
     def start(self):
@@ -319,10 +323,10 @@
 
     def copies(self, at, axis_of, source, target):
         made = []
-        for t in range(3):
-            axis = (t + axis_of) % 3
-            slot = self.here.slot[axis]
-            for k in range(1, RING):
+        for k in FAR_FIRST:
+            for t in range(3):
+                axis = (t + axis_of) % 3
+                slot = self.here.slot[axis]
                 made.append(
                     remote(
                         source(t, slot[k], slot[0]), target(t, k - 1, slot[0]),
@@ -748,6 +752,7 @@
 def finish_kernel(*refs):
     count = len(refs) // 2
     copies = [pltpu.make_async_copy(refs[i], refs[count + i], refs[-1].at[i]) for i in range(count)]
+    copies.sort(key=lambda copy: -math.prod(copy.src_ref.shape))
     begin(copies)
     end(copies)
 

time: 51.7 us -> 51.8 us (level)
  no operation moved by 1% of the time
where the time goes in v8:
time: 51.8 us; the launch traced here: 51.7 us
  Pallas kernels  50.8 us (98%)
  between operations  0.82 us (2%)
    pallas_call x1, Pallas kernels, per_device(): pl.pallas_call(functools.partial(block_kernel, n_lon, n_lat), out_shape=o...  49.2 us
    pallas_call x1, Pallas kernels, per_device(): pl.pallas_call(finish_kernel, out_shape=outputs, in_specs=[vmem] * len(ou...  1.59 us

profile of v8, /device:TPU:1, one launch (start us, length us, event | category | flops | bytes accessed | tf_op | source)
XLA Modules:
  0.0 51.7 jit_solution(10986529753677040158)
XLA Ops:
  0.6 49.2 %block.1 = (bf16[12,6,8,192]{3,2,1,0:T(8,128)(2,1)S(1)}, bf16[12,6,8,192]{3,2,1,0:T(8,128)(2,1)S(1)}, f32[192,576]{1,0:T(8,128)S(1)}, f32[192,192]{1,0:T(8,128)S...) custom-call(bf16[12,6,8,192]{3,2,1,0:T(8,128)(2,1)} %refs_0_.1, ...), custom_call_target="tpu_custom_call" | custom-call | tf_op jit(solution)/shard_map/block/pallas_call | solution.py:782
  49.9 1.6 %finish.1 = (bf16[12,6,8,192]{3,2,1,0:T(8,128)(2,1)}, bf16[12,6,8,192]{3,2,1,0:T(8,128)(2,1)}, f32[192,576]{1,0:T(8,128)}, f32[192,192]{1,0:T(8,128)}, f32[192,7...) custom-call(bf16[12,6,8,192]{3,2,1,0:T(8,128)(2,1)S(1)} %get-tuple-element.21.refs_0_, ...), custom_call_target="tpu_custom_call" | custom-call | tf_op jit(solution)/shard_map/finish/pallas_call | solution.py:829

commit v9 on v8

--- a/solution.py
+++ b/solution.py
@@ -257,12 +257,12 @@
         for at, tile in enumerate(tiles_in(block), first):
             self.src[at // (8 * n1), at // (2 * n1) % RING, at // n1 % 2, at % n1] = tile
 
-    def phase(self, at):
+    def phase(self, at, thirds=(0, 1, 2)):
         here, made = self.here, []
         sems = self.send.at[at], self.recv.at[at]
         if at in (0, 3):
             for k in range(7):
-                for t in range(3):
+                for t in thirds:
                     device, slot, core = here.eight[t][k]
                     mine = self.out.at[t, here.slot[t][0], here.core]
                     if at == 0:
@@ -277,8 +277,8 @@
                     made.append(remote(mine, mine, *sems, here.along[axis][k]))
         return made
 
-    def start(self):
-        begin(self.phase(0))
+    def start(self, *thirds):
+        begin(self.phase(0, thirds))
 
     def step(self, at):
         like = self.r1 if at in (0, 3) else self.r1.at[pl.ds(0, 3)]
@@ -683,46 +683,47 @@
     early.start()
     backward(0)
     backward(1)
+    early.step(0)
     backward(2)
-    early.step(0)
     backward(3)
     norm = normed[...]
     late.put(jnp.concatenate([dot_tn(norm, cot_q[...]), dot_tn(norm, cot_k[...])], axis=1), 0)
+    late.start(0)
     c_proj = dot_tn(blended[...], cot_mid[...])
     late.put(jnp.concatenate([dot_tn(norm, cot_v[...]), c_proj], axis=1), 36)
-    late.start()
+    late.start(1, 2)
+    early.step(1)
     collapse_bias(0, WH, scores, strips)
     strip_sum.put(join_strips(strips, columns, index_rows))
     strip_sum.start()
-    early.step(1)
+    late.step(0)
     inputs_back(0)
     inputs_back(1)
-    late.step(0)
+    early.step(2)
     scatter(1, gw)
+    late.step(1)
+    strip_sum.step(0)
     scatter(0, ow)
-    early.step(2)
-    strip_sum.step(0)
-    late.step(1)
     early.step(3)
+    late.step(2)
     strip_sum.step(1)
-    late.step(2)
-    early.step(4)
     end(outward[1])
     for index in range(4):
         merge(grad_field, index, [unpack(out[1, index, part]) for part in range(2)])
+    early.step(4)
+    strip_sum.step(2)
+    finish_bias(strip_sum.get(), lanes, tall_table, bias)
     end(outward[0])
     for index in range(4):
         merge(out_field, index, [unpack(out[0, index, part]) for part in range(2)])
-    strip_sum.step(2)
-    finish_bias(strip_sum.get(), lanes, tall_table, bias)
-    early.step(5)
-    fc1[...] = joined(early.get()[:72], 6)
-    fc2[...] = joined(early.get()[72:], 6)
     late.step(3)
     qkv[:, 0:384] = joined(tiles_of(l_out)[:36], 3)
     right = joined(tiles_of(l_out)[36:], 3)
     qkv[:, 384:576] = right[:, 0:C]
     proj[...] = right[:, C:]
+    early.step(5)
+    fc1[...] = joined(early.get()[:72], 6)
+    fc2[...] = joined(early.get()[72:], 6)
 
 
 def joined(tiles, columns):

time: 51.8 us -> 49.8 us (0.961)
  Pallas kernels: 50.8 us -> 48.9 us
    pallas_call x1, Pallas kernels: 49.2 us -> 47.3 us  [per_device(): pl.pallas_call(functools.partial(block_kernel, n_lon, n_lat), out_shape=o...]
where the time goes in v9:
time: 49.8 us; the launch traced here: 49.7 us
  Pallas kernels  48.9 us (98%)
  between operations  0.82 us (2%)
    pallas_call x1, Pallas kernels, per_device(): pl.pallas_call(functools.partial(block_kernel, n_lon, n_lat), out_shape=o...  47.3 us
    pallas_call x1, Pallas kernels, per_device(): pl.pallas_call(finish_kernel, out_shape=outputs, in_specs=[vmem] * len(ou...  1.59 us

profile of v9, /device:TPU:1, one launch (start us, length us, event | category | flops | bytes accessed | tf_op | source)
XLA Modules:
  0.0 49.7 jit_solution(17984829007625112805)
XLA Ops:
  0.6 47.3 %block.1 = (bf16[12,6,8,192]{3,2,1,0:T(8,128)(2,1)S(1)}, bf16[12,6,8,192]{3,2,1,0:T(8,128)(2,1)S(1)}, f32[192,576]{1,0:T(8,128)S(1)}, f32[192,192]{1,0:T(8,128)S...) custom-call(bf16[12,6,8,192]{3,2,1,0:T(8,128)(2,1)} %refs_0_.1, ...), custom_call_target="tpu_custom_call" | custom-call | tf_op jit(solution)/shard_map/block/pallas_call | solution.py:783
  47.9 1.6 %finish.1 = (bf16[12,6,8,192]{3,2,1,0:T(8,128)(2,1)}, bf16[12,6,8,192]{3,2,1,0:T(8,128)(2,1)}, f32[192,576]{1,0:T(8,128)}, f32[192,192]{1,0:T(8,128)}, f32[192,7...) custom-call(bf16[12,6,8,192]{3,2,1,0:T(8,128)(2,1)S(1)} %get-tuple-element.21.refs_0_, ...), custom_call_target="tpu_custom_call" | custom-call | tf_op jit(solution)/shard_map/finish/pallas_call | solution.py:830

commit v10 on v9

--- a/solution.py
+++ b/solution.py
@@ -548,9 +548,9 @@
     greeted = here.greet()
     begin(loads[6:9])
     loads[0].wait()
+    chunks = [split(field, index) for index in range(3)]
     for index in range(3):
-        for part, chunk in enumerate(split(field, index)):
-            sent[part, index] = pack(chunk)
+        sent[0, index] = pack(chunks[index][0])
     greeted()
     inward = [
         halo(here, sent.at[i], came.at[i], halo_send.at[i], halo_recv.at[i], -1) for i in range(2)
@@ -560,6 +560,8 @@
         halo(here, back.at[i], out.at[i], halo_send.at[3 + i], halo_recv.at[3 + i], 1) for i in range(2)
     ]
     begin(inward[0])
+    for index in range(3):
+        sent[1, index] = pack(chunks[index][1])
     begin(inward[1])
     begin(loads[1:6])
     end(loads[6:9])
@@ -674,6 +676,7 @@
     end(loads[3:6])
     feed(0)
     feed(1)
+    scatter(0, ow)
     end(cot_inward)
     for part in range(2):
         uw[part * PAIR : (part + 1) * PAIR, :] = gather(1, part)
@@ -703,7 +706,6 @@
     scatter(1, gw)
     late.step(1)
     strip_sum.step(0)
-    scatter(0, ow)
     early.step(3)
     late.step(2)
     strip_sum.step(1)

time: 49.8 us -> 50.5 us (1.014)
  Pallas kernels: 48.9 us -> 49.5 us
    pallas_call x1, Pallas kernels: 47.3 us -> 48 us  [per_device(): pl.pallas_call(functools.partial(block_kernel, n_lon, n_lat), out_shape=o...]
where the time goes in v10:
time: 50.5 us; the launch traced here: 50.4 us
  Pallas kernels  49.5 us (98%)
  between operations  0.82 us (2%)
    pallas_call x1, Pallas kernels, per_device(): pl.pallas_call(functools.partial(block_kernel, n_lon, n_lat), out_shape=o...  48 us
    pallas_call x1, Pallas kernels, per_device(): pl.pallas_call(finish_kernel, out_shape=outputs, in_specs=[vmem] * len(ou...  1.59 us

profile of v10, /device:TPU:1, one launch (start us, length us, event | category | flops | bytes accessed | tf_op | source)
XLA Modules:
  0.0 50.4 jit_solution(3764959599797839013)
XLA Ops:
  0.6 48.0 %block.1 = (bf16[12,6,8,192]{3,2,1,0:T(8,128)(2,1)S(1)}, bf16[12,6,8,192]{3,2,1,0:T(8,128)(2,1)S(1)}, f32[192,576]{1,0:T(8,128)S(1)}, f32[192,192]{1,0:T(8,128)S...) custom-call(bf16[12,6,8,192]{3,2,1,0:T(8,128)(2,1)} %refs_0_.1, ...), custom_call_target="tpu_custom_call" | custom-call | tf_op jit(solution)/shard_map/block/pallas_call | solution.py:785
  48.6 1.6 %finish.1 = (bf16[12,6,8,192]{3,2,1,0:T(8,128)(2,1)}, bf16[12,6,8,192]{3,2,1,0:T(8,128)(2,1)}, f32[192,576]{1,0:T(8,128)}, f32[192,192]{1,0:T(8,128)}, f32[192,7...) custom-call(bf16[12,6,8,192]{3,2,1,0:T(8,128)(2,1)S(1)} %get-tuple-element.21.refs_0_, ...), custom_call_target="tpu_custom_call" | custom-call | tf_op jit(solution)/shard_map/finish/pallas_call | solution.py:832

commit v11 on v9

--- a/solution.py
+++ b/solution.py
@@ -63,17 +63,12 @@
     return ((SHIFTS - 1 - d) * SITE + lev * WLAT + a).reshape(STRIP).astype(np.int32)
 
 
-def row_places():
-    wh, _, site = np.meshgrid(np.arange(WH), np.arange(2), np.arange(SITE), indexing="ij")
-    return (site * WH + wh).reshape(WH * 2 * SITE).astype(np.int32)
-
-
 def row_codes():
-    _, w, p, lev, a = np.meshgrid(
-        np.arange(HEADS), np.arange(LWIN), np.arange(2), np.arange(WLEV), np.arange(WLAT), indexing="ij"
+    lev, a, _, w = np.meshgrid(
+        np.arange(WLEV), np.arange(WLAT), np.arange(HEADS), np.arange(LWIN), indexing="ij"
     )
-    code = lev + 2 * (a >= WLAT // 2) + 4 * (w == LWIN - 1) + 8 * (p == 0)
-    return code.reshape(WH * 2 * SITE).astype(np.int32)
+    code = lev + 2 * (a >= WLAT // 2) + 4 * (w == LWIN - 1)
+    return code.reshape(SITE * WH).astype(np.int32)
 
 
 def lane_codes():
@@ -482,29 +477,27 @@
             gathered[site * WH : (site + 1) * WH, other * RUN : (other + 1) * RUN] = tall_table[
                 :, start : start + RUN
             ]
-    moved = sum(dot(part, lanes[...]) for part in pieces(gathered[...], 3))
-    rows = one_hot(columns[:, 1:2], WH * 2 * SITE, SITE * WH)
-    moved = sum(dot(rows, part) for part in pieces(moved, 3))
-    code = columns[:, 2:3]
-    moved = jnp.where((code & 8) != 0, pltpu.roll(moved, LANES - SITE, 1), moved) * LOG2E
+    strip = sum(dot(part, lanes[...]) for part in pieces(gathered[...], 3)) * LOG2E
+    code = columns[0 : SITE * WH, 2:3]
     seen = jnp.where((code & 4) != 0, 1, 0) + jnp.where(last_lat, 2, 0)
     apart = (code ^ index_rows[2:3, 0:LANES]) & seen
-    strips[...] = jnp.where(apart != 0, MASKED, moved)
+    strip = jnp.where(apart != 0, MASKED, strip)
+    for c in range(LANES // 128):
+        strips[c] = strip[:, c * 128 : (c + 1) * 128]
 
     def one(wh, carry):
-        strip = strips[pl.ds(pl.multiple_of(wh * 2 * SITE, 8), 2 * SITE), :]
+        odd = jnp.concatenate([strips[c, pl.ds(wh, SITE, WH), :] for c in range(LANES // 128)], axis=1)
+        both = jnp.concatenate([pltpu.roll(odd, LANES - SITE, 1), odd], axis=0)
         start = lax.rem(wh, LWIN) * STACK + lax.div(wh, LWIN) * WIN
         for pair in range(WLON // 2):
             offset = (WLON - 2 - 2 * pair) * SITE
-            scores[pl.ds(pl.multiple_of(start + pair * 24, 8), 24), :] = strip[
-                :, offset : offset + WIN
-            ]
+            scores[pl.ds(pl.multiple_of(start + pair * 24, 8), 24), :] = both[:, offset : offset + WIN]
         return carry
 
     lax.fori_loop(0, WH, one, 0)
 
 
-def collapse_bias(first, last, scores, strips):
+def collapse_bias(scores, strips):
     def one(wh, carry):
         start = lax.rem(wh, LWIN) * STACK + lax.div(wh, LWIN) * WIN
         total = jnp.zeros((2 * SITE, LANES), F32)
@@ -513,17 +506,12 @@
             part = scores[pl.ds(pl.multiple_of(start + pair * 24, 8), 24), :]
             part = jnp.concatenate([part, jnp.zeros((2 * SITE, LANES - WIN), F32)], axis=1)
             total = total + (pltpu.roll(part, offset, 1) if offset else part)
-        strips[pl.ds(pl.multiple_of(wh * 2 * SITE, 8), 2 * SITE), :] = total
+        total = pltpu.roll(total[:SITE], SITE, 1) + total[SITE:]
+        for c in range(LANES // 128):
+            strips[c, pl.ds(wh, SITE, WH), :] = total[:, c * 128 : (c + 1) * 128]
         return carry
 
-    lax.fori_loop(first, last, one, 0)
-
-
-def join_strips(strips, columns, index_rows):
-    total = strips[...]
-    total = jnp.where((columns[:, 2:3] & 8) != 0, pltpu.roll(total, SITE, 1), total)
-    rows = one_hot(index_rows[1:2, :], SITE * WH, WH * 2 * SITE)
-    return sum(dot(rows, part) for part in pieces(total, 2))
+    lax.fori_loop(0, WH, one, 0)
 
 
 def block_kernel(n_lon, n_lat, *refs):
@@ -693,8 +681,8 @@
     late.put(jnp.concatenate([dot_tn(norm, cot_v[...]), c_proj], axis=1), 36)
     late.start(1, 2)
     early.step(1)
-    collapse_bias(0, WH, scores, strips)
-    strip_sum.put(join_strips(strips, columns, index_rows))
+    collapse_bias(scores, strips)
+    strip_sum.put(jnp.concatenate([strips[c] for c in range(LANES // 128)], axis=1))
     strip_sum.start()
     late.step(0)
     inputs_back(0)
@@ -762,9 +750,8 @@
     vmem, hbm = pl.BlockSpec(memory_space=pltpu.VMEM), pl.BlockSpec(memory_space=pltpu.HBM)
     shape = jax.ShapeDtypeStruct
     dma = pltpu.SemaphoreType.DMA
-    rows = row_places()
-    columns = columns_of(token_places(), rows, row_codes(), lane_places())
-    index_rows = columns_of(token_places(), rows, lane_codes()).T.copy()
+    columns = columns_of(token_places(), [], row_codes(), lane_places())
+    index_rows = columns_of(token_places(), [], lane_codes()).T.copy()
     inputs = (
         field, cotangent, w_qkv, w_proj, w_fc1, w_fc2.T, bias_table[0].transpose(1, 0, 2), columns, index_rows
     )
@@ -810,7 +797,7 @@
             *wide(BF16, 6),
             pltpu.VMEM((WH, POS), F32),
             pltpu.VMEM((SITE * WH, STRIP), F32),
-            pltpu.VMEM((WH * 2 * SITE, LANES), F32),
+            pltpu.VMEM((LANES // 128, SITE * WH, 128), F32),
             pltpu.VMEM((3, C, C), BF16),
             pltpu.VMEM((PAIR, PAIR), BF16),
             pltpu.VMEM((PAIR, PAIR), BF16),

time: 49.8 us -> 50.4 us (1.012)
  Pallas kernels: 48.9 us -> 49.7 us
    pallas_call x1, Pallas kernels: 47.3 us -> 48.1 us  [per_device(): pl.pallas_call(functools.partial(block_kernel, n_lon, n_lat), out_shape=o...]
where the time goes in v11:
time: 50.4 us; the launch traced here: 50.3 us
  Pallas kernels  49.7 us (99%)
  between operations  0.64 us (1%)
    pallas_call x1, Pallas kernels, per_device(): pl.pallas_call(functools.partial(block_kernel, n_lon, n_lat), out_shape=o...  48.1 us
    pallas_call x1, Pallas kernels, per_device(): pl.pallas_call(finish_kernel, out_shape=outputs, in_specs=[vmem] * len(ou...  1.59 us

profile of v11, /device:TPU:1, one launch (start us, length us, event | category | flops | bytes accessed | tf_op | source)
XLA Modules:
  0.0 50.3 jit_solution(11042421217637903072)
XLA Ops:
  0.6 48.1 %block.1 = (bf16[12,6,8,192]{3,2,1,0:T(8,128)(2,1)S(1)}, bf16[12,6,8,192]{3,2,1,0:T(8,128)(2,1)S(1)}, f32[192,576]{1,0:T(8,128)S(1)}, f32[192,192]{1,0:T(8,128)S...) custom-call(bf16[12,6,8,192]{3,2,1,0:T(8,128)(2,1)} %refs_0_.1, ...), custom_call_target="tpu_custom_call" | custom-call | tf_op jit(solution)/shard_map/block/pallas_call | solution.py:770
  48.7 1.6 %finish.1 = (bf16[12,6,8,192]{3,2,1,0:T(8,128)(2,1)}, bf16[12,6,8,192]{3,2,1,0:T(8,128)(2,1)}, f32[192,576]{1,0:T(8,128)}, f32[192,192]{1,0:T(8,128)}, f32[192,7...) custom-call(bf16[12,6,8,192]{3,2,1,0:T(8,128)(2,1)S(1)} %get-tuple-element.21.refs_0_, ...), custom_call_target="tpu_custom_call" | custom-call | tf_op jit(solution)/shard_map/finish/pallas_call | solution.py:817
